TPU v7x, 256 devices: a whole 4x4x8 slice. The times are simulated.
256 devices in a mesh: dom: 8 (over x, core), fsdp: 32 (over y, z).
Axes of the slice: x: 4, y: 4, z: 8, core: 2. Of those that a mesh axis runs over, the one named last changes fastest.
Arguments:
- node_state: bfloat16 [196608, 256], P(('dom', 'fsdp')), may hold values from -6 to 6
- edge_state: bfloat16 [524288, 256], P(('dom', 'fsdp')), may hold values from -6 to 6
- cotangent: bfloat16 [196608, 256], P(('dom', 'fsdp')), may hold values from -6 to 6
- w_first: bfloat16 [768, 256], P('fsdp'), may hold values from -0.21875 to 0.21875
- w_second: bfloat16 [256, 256], P('fsdp'), may hold values from -0.375 to 0.375
- w_third: bfloat16 [256, 256], P('fsdp'), may hold values from -0.375 to 0.375
- pair_near: int32 [4096], P(('dom', 'fsdp')), may hold values from 0 to 5
- pair_far: int32 [4096], P(('dom', 'fsdp')), may hold values from 0 to 9, as said below
- send_fsdp: int32 [256, 2, 1], P(('dom', 'fsdp')), may hold values from 0 to 5
- send_dom: int32 [256, 2, 1], P(('dom', 'fsdp')), may hold values from 0 to 5
Outputs:
- new_state: bfloat16 [196608, 256], P(('dom', 'fsdp'))
- grad_state: bfloat16 [196608, 256], P(('dom', 'fsdp'))
- grad_edges: bfloat16 [524288, 256], P(('dom', 'fsdp'))
- grad_first: float32 [768, 256], P('fsdp')
- grad_second: float32 [256, 256], P('fsdp')
- grad_third: float32 [256, 256], P('fsdp')
Inputs may be any that keep to these rules, and one draw needn't show every extreme that they name: `pair_near`: an own block of the holding device. `pair_far`: an entry of the holding device's extended table; each entry from 6 on is named by exactly one pair of the holding device, the other pairs name own blocks. `send_fsdp`: an own block of the lending device. `send_dom`: an own block of the lending device.
All inputs are finite; a program needn't handle non-finite values.
Results may differ from a plain program's by a relative error of at most 0.024.
Values may be sent and summed in bfloat16 or wider, within the bound.
A program may use at most 64 MiB of HBM per device.

v0:
```python
import jax
import jax.numpy as jnp
from jax import lax
from jax.sharding import PartitionSpec as P

BLOCK = 128


def extended(cells, sides, width):
    for axis, dim in sides:
        count = lax.axis_size(axis)
        head = lax.slice_in_dim(cells, 0, width, axis=dim)
        tail = lax.slice_in_dim(cells, cells.shape[dim] - width, cells.shape[dim], axis=dim)
        cells = jnp.concatenate(
            [
                lax.ppermute(tail, axis, [(i, (i + 1) % count) for i in range(count)]),
                cells,
                lax.ppermute(head, axis, [((i + 1) % count, i) for i in range(count)]),
            ],
            axis=dim,
        )
    return cells


def silu_slope(values):
    sigmoid = jax.nn.sigmoid(values)
    return sigmoid * (1.0 + values * (1.0 - sigmoid))


def forward_pass(near_rows, far_rows, edge_rows, w_first, w_second, w_third):
    edge_count = near_rows.shape[0]
    stacked = jnp.concatenate(
        [
            jnp.concatenate([near_rows, far_rows, edge_rows], 1),
            jnp.concatenate([far_rows, near_rows, edge_rows], 1),
        ],
        0,
    )
    first_pre = jnp.dot(stacked, w_first, preferred_element_type=jnp.float32)
    first_act = jax.nn.silu(first_pre).astype(jnp.bfloat16)
    second_pre = jnp.dot(first_act, w_second, preferred_element_type=jnp.float32)
    second_act = jax.nn.silu(second_pre).astype(jnp.bfloat16)
    message = jnp.dot(second_act, w_third, preferred_element_type=jnp.float32)
    face_flux = message[:edge_count] - message[edge_count:]
    return (face_flux, (stacked, first_pre, first_act, second_pre, second_act))


def backward_pass(flux_grad, saved, w_first, w_second, w_third):
    stacked, first_pre, first_act, second_pre, second_act = saved
    edge_count = flux_grad.shape[0]
    latent = w_second.shape[0]
    signed = flux_grad.astype(jnp.bfloat16)
    both_grad = jnp.concatenate([signed, -signed], 0)
    second_grad = (
        jnp.dot(both_grad, w_third.T, preferred_element_type=jnp.float32) * silu_slope(second_pre)
    ).astype(jnp.bfloat16)
    first_grad = (
        jnp.dot(second_grad, w_second.T, preferred_element_type=jnp.float32) * silu_slope(first_pre)
    ).astype(jnp.bfloat16)
    forward_part = first_grad[:edge_count]
    mirror_part = first_grad[edge_count:]

    def through(row_block, offset):
        return jnp.dot(
            row_block, w_first[offset : offset + latent].T, preferred_element_type=jnp.float32
        )

    near_grad = through(forward_part, 0) + through(mirror_part, latent)
    far_grad = through(forward_part, latent) + through(mirror_part, 0)
    edge_grad = (through(forward_part, 2 * latent) + through(mirror_part, 2 * latent)).astype(
        jnp.bfloat16
    )
    grad_third = jnp.dot(second_act.T, both_grad, preferred_element_type=jnp.float32)
    grad_second = jnp.dot(first_act.T, second_grad, preferred_element_type=jnp.float32)
    grad_first = jnp.dot(stacked.T, first_grad, preferred_element_type=jnp.float32)
    return (near_grad, far_grad, edge_grad, (grad_first, grad_second, grad_third))


def spread(values, row_index, count_rows):
    onehot = (row_index[None, :] == jnp.arange(count_rows, dtype=jnp.int32)[:, None]).astype(
        jnp.float32
    )
    flattened = values.reshape(values.shape[0], -1)
    summed = jnp.dot(onehot, flattened, precision=lax.Precision.HIGHEST)
    return summed.reshape(count_rows, values.shape[1], values.shape[2])


def outer_rims(padded, width):
    return jnp.concatenate([padded[:width], padded[padded.shape[0] - width :]], 0)


def back_fsdp(rims, width):
    padded = extended(rims, (("fsdp", 0),), width)
    return outer_rims(padded, width)


def back_dom(rims, width):
    padded = extended(rims, (("dom", 0),), width)
    return outer_rims(padded, width)


def owner_sum(received, block_list, local_count):
    return spread(received.astype(jnp.float32), block_list.reshape(-1), local_count)


def body(
    node_state,
    edge_state,
    cotangent,
    w_first,
    w_second,
    w_third,
    pair_near,
    pair_far,
    send_fsdp,
    send_dom,
):
    latent = node_state.shape[1]
    local_count = node_state.shape[0] // BLOCK
    node_blocks = node_state.reshape(local_count, BLOCK, latent)
    cot_blocks = cotangent.reshape(local_count, BLOCK, latent)
    list_fsdp = send_fsdp[0]
    list_dom = send_dom[0]
    width_fsdp = list_fsdp.shape[1]
    width_dom = list_dom.shape[1]
    full_first, full_second, full_third = (
        lax.all_gather(w_first, "fsdp", axis=0, tiled=True),
        lax.all_gather(w_second, "fsdp", axis=0, tiled=True),
        lax.all_gather(w_third, "fsdp", axis=0, tiled=True),
    )
    ids_fsdp = list_fsdp.reshape(-1)
    ids_dom = list_dom.reshape(-1)
    lend_fsdp = jnp.stack([node_blocks[ids_fsdp], cot_blocks[ids_fsdp]], 1)
    lend_dom = jnp.stack([node_blocks[ids_dom], cot_blocks[ids_dom]], 1)
    recv_fsdp = outer_rims(extended(lend_fsdp, (("fsdp", 0),), width_fsdp), width_fsdp)
    recv_dom = outer_rims(extended(lend_dom, (("dom", 0),), width_dom), width_dom)
    state_table = jnp.concatenate([node_blocks, recv_fsdp[:, 0], recv_dom[:, 0]], 0)
    cot_table = jnp.concatenate([cot_blocks, recv_fsdp[:, 1], recv_dom[:, 1]], 0)
    table_count = state_table.shape[0]
    rims_end = local_count + 2 * width_fsdp
    near_rows = node_blocks[pair_near].reshape(-1, latent)
    far_rows = state_table[pair_far].reshape(-1, latent)
    face_flux, saved = forward_pass(
        near_rows, far_rows, edge_state, full_first, full_second, full_third
    )
    flux_blocks = face_flux.reshape(-1, BLOCK, latent)
    near_state = spread(flux_blocks, pair_near, local_count)
    far_state = spread(-flux_blocks, pair_far, table_count)
    state_fsdp = far_state[local_count:rims_end].astype(jnp.bfloat16)
    state_dom = far_state[rims_end:].astype(jnp.bfloat16)
    state_back_fsdp = back_fsdp(state_fsdp, width_fsdp)
    state_back_dom = back_dom(state_dom, width_dom)
    flux_grad = (
        cot_blocks[pair_near].astype(jnp.float32) - cot_table[pair_far].astype(jnp.float32)
    ).reshape(-1, latent)
    near_grad, far_grad, edge_grad, grads = backward_pass(
        flux_grad, saved, full_first, full_second, full_third
    )
    near_back = spread(near_grad.reshape(-1, BLOCK, latent), pair_near, local_count)
    far_back = spread(far_grad.reshape(-1, BLOCK, latent), pair_far, table_count)
    grad_fsdp = far_back[local_count:rims_end].astype(jnp.bfloat16)
    grad_dom = far_back[rims_end:].astype(jnp.bfloat16)
    grad_back_fsdp = back_fsdp(grad_fsdp, width_fsdp)
    grad_back_dom = back_dom(grad_dom, width_dom)
    state_total = node_blocks.astype(jnp.float32) + near_state + far_state[:local_count]
    state_total = (
        state_total
        + owner_sum(state_back_fsdp, list_fsdp, local_count)
        + owner_sum(state_back_dom, list_dom, local_count)
    )
    grad_total = cot_blocks.astype(jnp.float32) + near_back + far_back[:local_count]
    grad_total = (
        grad_total
        + owner_sum(grad_back_fsdp, list_fsdp, local_count)
        + owner_sum(grad_back_dom, list_dom, local_count)
    )
    new_state = state_total.astype(jnp.bfloat16).reshape(-1, latent)
    grad_state = grad_total.astype(jnp.bfloat16).reshape(-1, latent)
    whole = (
        lax.psum(grads[0].astype(jnp.bfloat16), "dom").astype(jnp.float32),
        lax.psum(grads[1].astype(jnp.bfloat16), "dom").astype(jnp.float32),
        lax.psum(grads[2].astype(jnp.bfloat16), "dom").astype(jnp.float32),
    )
    totals = (
        lax.psum_scatter(
            whole[0].astype(jnp.bfloat16), "fsdp", scatter_dimension=0, tiled=True
        ).astype(jnp.float32),
        lax.psum_scatter(
            whole[1].astype(jnp.bfloat16), "fsdp", scatter_dimension=0, tiled=True
        ).astype(jnp.float32),
        lax.psum_scatter(
            whole[2].astype(jnp.bfloat16), "fsdp", scatter_dimension=0, tiled=True
        ).astype(jnp.float32),
    )
    return (new_state, grad_state, edge_grad, totals[0], totals[1], totals[2])


def solution(mesh):
    return jax.shard_map(
        body,
        mesh=mesh,
        in_specs=(
            P(("dom", "fsdp"), None),
            P(("dom", "fsdp"), None),
            P(("dom", "fsdp"), None),
            P("fsdp", None),
            P("fsdp", None),
            P("fsdp", None),
            P(("dom", "fsdp")),
            P(("dom", "fsdp")),
            P(("dom", "fsdp"), None, None),
            P(("dom", "fsdp"), None, None),
        ),
        out_specs=(
            P(("dom", "fsdp"), None),
            P(("dom", "fsdp"), None),
            P(("dom", "fsdp"), None),
            P("fsdp", None),
            P("fsdp", None),
            P("fsdp", None),
        ),
        check_vma=False,
    )
```

profile of v0, /device:TPU:1, one launch (start us, length us, event | category | flops | bytes accessed | tf_op | source)
XLA Modules:
  0.0 849.7 jit_solution(4839243657522487174)
XLA Ops:
  11.8 3.3 collective-permute-start.3
  19.5 7.5 collective-permute-start.1
  27.0 36.0 %all_gather.10 = bf16[256,256]{1,0:T(8,128)(2,1)} all-gather(bf16[8,256]{1,0:T(8,128)(2,1)S(1)} %copy-done.17), channel_id=1, replica_groups=mesh['dom'=8,'fsdp'=32] {'fsdp'}, dimensions={0}, use_global_device_ids=true | all-gather | bytes 135168 | tf_op jit(solution)/shard_map/all_gather | solution.py:128
  63.0 40.3 %all_gather.9 = bf16[768,256]{1,0:T(8,128)(2,1)} all-gather(bf16[24,256]{1,0:T(8,128)(2,1)S(1)} %copy-done.16), channel_id=1, replica_groups=mesh['dom'=8,'fsdp'=32] {'fsdp'}, dimensions={0}, use_global_device_ids=true | all-gather | bytes 405504 | tf_op jit(solution)/shard_map/all_gather | solution.py:127
  103.3 35.4 %all_gather.11 = bf16[256,256]{1,0:T(8,128)(2,1)} all-gather(bf16[8,256]{1,0:T(8,128)(2,1)S(1)} %copy-done.18), channel_id=1, replica_groups=mesh['dom'=8,'fsdp'=32] {'fsdp'}, dimensions={0}, use_global_device_ids=true | all-gather | bytes 135168 | tf_op jit(solution)/shard_map/all_gather | solution.py:129
  148.1 27.2 %multiply_convert_fusion.1 = (bf16[4096,256]{1,0:T(8,128)(2,1)S(1)}, f32[4096,256]{1,0:T(8,128)}) fusion(bf16[768,256]{1,0:T(8,128)(2,1)S(1)} %copy-done.8, bf16[2048,256]{1,0:T(8,128)(2,1)S(1)} %copy-done.23, bf16[2048,256]{1,0:T(8,128)(2,1)S(1)} %bitcast.141, bf16[2048,256]{1,0:T(8,128)(2,1)S(1)} %bitcast.143), kind=kOutput, calls=%fused_computation.15 | convolution fusion | flops 1653604352 | bytes 9830400 | tf_op jit(solution)/shard_map/dot_general | solution.py:39
  175.4 3.2 multiply_convert_fusion
  178.6 2.6 fusion.95
  182.6 4.3 fusion
  189.8 4.7 fusion.1
  202.8 3.8 slice_subtract_fusion
  208.3 3.7 convolution_add_fusion.1
  212.0 2.7 reshape_reshape.11
  214.8 4.0 fusion.86
  222.5 33.2 %collective-permute-start.10 = (bf16[1,128,256]{2,1,0:T(8,128)(2,1)S(1)}, bf16[1,128,256]{2,1,0:T(8,128)(2,1)S(1)}, u32[]{:S(2)}, u32[]{:S(2)}) collective-permute-start(bf16[1,128,256]{2,1,0:T(8,128)(2,1)S(1)} %slice.159), channel_id=1, source_target_pairs={{0,32},{32,64},{64,96},{96,128},{128,160},{160,192},{192,224},{224... | collective-permute-start | bytes 196616 | tf_op jit(solution)/shard_map/ppermute | solution.py:16
  256.2 3.8 convolution_add_fusion.2
  260.0 2.8 fusion.85
  264.3 3.0 slice_reduce_fusion.7
  269.6 2.8 reshape_reshape.10
  272.5 4.8 collective-permute-start.5
  295.1 121.7 %reduce-scatter.8.cloned.1.call-done = bf16[8,256]{1,0:T(8,128)(2,1)} async-done(((bf16[256,256]{1,0:T(8,128)(2,1)}), bf16[8,256]{1,0:T(8,128)(2,1)}) %reduce-scatter.8.cloned.1.call-update) | async-done | bytes 4112 | tf_op jit(solution)/shard_map/reduce_scatter | solution.py:191
  416.7 194.9 %reduce-scatter.6.cloned.1.call-done = bf16[8,256]{1,0:T(8,128)(2,1)} async-done(((bf16[256,256]{1,0:T(8,128)(2,1)}), bf16[8,256]{1,0:T(8,128)(2,1)}) %reduce-scatter.6.cloned.1.call-update) | async-done | bytes 4112 | tf_op jit(solution)/shard_map/reduce_scatter | solution.py:188
  611.7 203.0 %reduce-scatter.4.cloned.1.call-done = bf16[24,256]{1,0:T(8,128)(2,1)} async-done(((bf16[768,256]{1,0:T(8,128)(2,1)}), bf16[24,256]{1,0:T(8,128)(2,1)}) %reduce-scatter.4.cloned.1.call-update) | async-done | bytes 12304 | tf_op jit(solution)/shard_map/reduce_scatter | solution.py:185
  814.7 26.6 %all-reduce = (bf16[24,256]{1,0:T(8,128)(2,1)S(1)}, bf16[8,256]{1,0:T(8,128)(2,1)S(1)}, bf16[8,256]{1,0:T(8,128)(2,1)S(1)}) all-reduce(bf16[24,256]{1,0:T(8,128)(2,1)} %reduce-scatter.4.cloned.1.call-done, bf16[8,256]{1,0:T(8,128)(2,1)} %reduce-scatter.6.cloned.1.call-done, ...), channel_id=1, replica_groups=mesh['dom'=8,'fsdp'=32] {'dom'}, use_global_device_ids=true, to_apply=%region_0.1 | all-reduce | flops 10240 | bytes 40960 | tf_op jit(solution)/shard_map/psum | solution.py:180
  (142 shorter events, 60.0 us)
Async XLA Ops:
  7.2 131.5 %copy-start.3 = (bf16[768,256]{1,0:T(8,128)(2,1)S(1)}, bf16[768,256]{1,0:T(8,128)(2,1)}, u32[]{:S(2)}) copy-start(bf16[768,256]{1,0:T(8,128)(2,1)} %param.12) | copy-start | bytes 1179652
  7.2 19.8 %copy-start.17 = (bf16[8,256]{1,0:T(8,128)(2,1)S(1)}, bf16[8,256]{1,0:T(8,128)(2,1)}, u32[]{:S(2)}) copy-start(bf16[8,256]{1,0:T(8,128)(2,1)} %param.14) | copy-start | bytes 12292
  7.2 55.8 %copy-start.16 = (bf16[24,256]{1,0:T(8,128)(2,1)S(1)}, bf16[24,256]{1,0:T(8,128)(2,1)}, u32[]{:S(2)}) copy-start(bf16[24,256]{1,0:T(8,128)(2,1)} %param.13) | copy-start | bytes 36868
  7.2 96.1 %copy-start.18 = (bf16[8,256]{1,0:T(8,128)(2,1)S(1)}, bf16[8,256]{1,0:T(8,128)(2,1)}, u32[]{:S(2)}) copy-start(bf16[8,256]{1,0:T(8,128)(2,1)} %param.15) | copy-start | bytes 12292
  7.2 409.5 %reduce-scatter.8.cloned.1.call-start = ((), (), s32[]{:S(2)}) async-start(), calls=%async_computation.5 | async-start | bytes 135168 | tf_op jit(solution)/shard_map/reduce_scatter | solution.py:191
  11.7 127.6 %copy-start.2 = (bf16[768,256]{1,0:T(8,128)(2,1)S(1)}, bf16[768,256]{1,0:T(8,128)(2,1)}, u32[]{:S(2)}) copy-start(bf16[768,256]{1,0:T(8,128)(2,1)} %param.10) | copy-start | bytes 1179652
  11.8 129.2 %collective-permute-start.3 = (bf16[1,2,128,256]{3,2,0,1:T(8,128)(2,1)S(1)}, bf16[1,2,128,256]{3,2,0,1:T(8,128)(2,1)S(1)}, u32[]{:S(2)}, u32[]{:S(2)}) collective-permute-start(bf16[1,2,128,256]{3,2,0,1:T(8,128)(2,1)S(1)} %get-tuple-element.23), channel_id=1, source_target_pairs={{32,0},{64,32},{96,64},{128,96},{160,128},{192,160},{224,192},{0,2... | collective-permute-start | bytes 393224 | tf_op jit(solution)/shard_map/ppermute | solution.py:18
  15.0 125.9 %collective-permute-start.2 = (bf16[1,2,128,256]{3,2,0,1:T(8,128)(2,1)S(1)}, bf16[1,2,128,256]{3,2,0,1:T(8,128)(2,1)S(1)}, u32[]{:S(2)}, u32[]{:S(2)}) collective-permute-start(bf16[1,2,128,256]{3,2,0,1:T(8,128)(2,1)S(1)} %get-tuple-element.24), channel_id=1, source_target_pairs={{0,32},{32,64},{64,96},{96,128},{128,160},{160,192},{192,224},{224... | collective-permute-start | bytes 393224 | tf_op jit(solution)/shard_map/ppermute | solution.py:16
  19.5 122.1 %collective-permute-start.1 = (bf16[1,2,128,256]{3,2,0,1:T(8,128)(2,1)S(1)}, bf16[1,2,128,256]{3,2,0,1:T(8,128)(2,1)S(1)}, u32[]{:S(2)}, u32[]{:S(2)}) collective-permute-start(bf16[1,2,128,256]{3,2,0,1:T(8,128)(2,1)S(1)} %get-tuple-element.21), channel_id=1, source_target_pairs={{1,0},{2,1},{3,2},{4,3},{5,4},{6,5},{7,6},{8,7},{9,8},{10,9},{11,1... | collective-permute-start | bytes 393224 | tf_op jit(solution)/shard_map/ppermute | solution.py:18
  27.0 114.6 %collective-permute-start = (bf16[1,2,128,256]{3,2,0,1:T(8,128)(2,1)S(1)}, bf16[1,2,128,256]{3,2,0,1:T(8,128)(2,1)S(1)}, u32[]{:S(2)}, u32[]{:S(2)}) collective-permute-start(bf16[1,2,128,256]{3,2,0,1:T(8,128)(2,1)S(1)} %get-tuple-element.22), channel_id=1, source_target_pairs={{0,1},{1,2},{2,3},{3,4},{4,5},{5,6},{6,7},{7,8},{8,9},{9,10},{10,1... | collective-permute-start | bytes 393224 | tf_op jit(solution)/shard_map/ppermute | solution.py:16
  146.1 35.1 %copy-start.7 = (bf16[16,128,256]{2,1,0:T(8,128)(2,1)}, bf16[16,128,256]{2,1,0:T(8,128)(2,1)S(1)}, u32[]{:S(2)}) copy-start(bf16[16,128,256]{2,1,0:T(8,128)(2,1)S(1)} %subtract_convert_fusion) | copy-start | bytes 3145732
  148.1 27.2 %copy-start.15 = (bf16[256,256]{1,0:T(8,128)(2,1)S(1)}, bf16[256,256]{1,0:T(8,128)(2,1)}, u32[]{:S(2)}) copy-start(bf16[256,256]{1,0:T(8,128)(2,1)} %all_gather.10) | copy-start | bytes 393220
  202.7 409.0 %reduce-scatter.6.cloned.1.call-start = ((), (), s32[]{:S(2)}) async-start(), calls=%async_computation.4 | async-start | bytes 135168 | tf_op jit(solution)/shard_map/reduce_scatter | solution.py:188
  221.0 58.7 %collective-permute-start.9 = (bf16[1,128,256]{2,1,0:T(8,128)(2,1)S(1)}, bf16[1,128,256]{2,1,0:T(8,128)(2,1)}, u32[]{:S(2)}, u32[]{:S(2)}) collective-permute-start(bf16[1,128,256]{2,1,0:T(8,128)(2,1)S(1)} %slice.157), channel_id=1, source_target_pairs={{1,0},{2,1},{3,2},{4,3},{5,4},{6,5},{7,6},{8,7},{9,8},{10,9},{11,1... | collective-permute-start | bytes 196616 | tf_op jit(solution)/shard_map/ppermute | solution.py:18
  222.5 62.1 %collective-permute-start.10 = (bf16[1,128,256]{2,1,0:T(8,128)(2,1)S(1)}, bf16[1,128,256]{2,1,0:T(8,128)(2,1)S(1)}, u32[]{:S(2)}, u32[]{:S(2)}) collective-permute-start(bf16[1,128,256]{2,1,0:T(8,128)(2,1)S(1)} %slice.159), channel_id=1, source_target_pairs={{0,32},{32,64},{64,96},{96,128},{128,160},{160,192},{192,224},{224... | collective-permute-start | bytes 196616 | tf_op jit(solution)/shard_map/ppermute | solution.py:16
  255.7 29.2 %collective-permute-start.11 = (bf16[1,128,256]{2,1,0:T(8,128)(2,1)S(1)}, bf16[1,128,256]{2,1,0:T(8,128)(2,1)}, u32[]{:S(2)}, u32[]{:S(2)}) collective-permute-start(bf16[1,128,256]{2,1,0:T(8,128)(2,1)S(1)} %slice.161), channel_id=1, source_target_pairs={{32,0},{64,32},{96,64},{128,96},{160,128},{192,160},{224,192},{0,2... | collective-permute-start | bytes 196616 | tf_op jit(solution)/shard_map/ppermute | solution.py:18
  256.2 25.3 %collective-permute-start.8 = (bf16[1,128,256]{2,1,0:T(8,128)(2,1)}, bf16[1,128,256]{2,1,0:T(8,128)(2,1)}, u32[]{:S(2)}, u32[]{:S(2)}) collective-permute-start(bf16[1,128,256]{2,1,0:T(8,128)(2,1)} %slice.155), channel_id=1, source_target_pairs={{0,1},{1,2},{2,3},{3,4},{4,5},{5,6},{6,7},{7,8},{8,9},{9,10},{10,1... | collective-permute-start | bytes 196616 | tf_op jit(solution)/shard_map/ppermute | solution.py:16
  264.3 550.4 %reduce-scatter.4.cloned.1.call-start = ((), (), s32[]{:S(2)}) async-start(), calls=%async_computation.3 | async-start | bytes 405504 | tf_op jit(solution)/shard_map/reduce_scatter | solution.py:185
  272.4 11.8 %copy-start.19 = (s32[1,2,1]{1,2,0:T(1,128)S(1)}, s32[1,2,1]{1,2,0:T(1,128)}, u32[]{:S(2)}) copy-start(s32[1,2,1]{1,2,0:T(1,128)} %param.18) | copy-start | bytes 28
  272.5 16.2 %collective-permute-start.5 = (bf16[1,128,256]{2,1,0:T(8,128)(2,1)S(1)}, bf16[1,128,256]{2,1,0:T(8,128)(2,1)S(1)}, u32[]{:S(2)}, u32[]{:S(2)}) collective-permute-start(bf16[1,128,256]{2,1,0:T(8,128)(2,1)S(1)} %slice.141), channel_id=1, source_target_pairs={{1,0},{2,1},{3,2},{4,3},{5,4},{6,5},{7,6},{8,7},{9,8},{10,9},{11,1... | collective-permute-start | bytes 196616 | tf_op jit(solution)/shard_map/ppermute | solution.py:18
  277.4 8.4 copy-start.20
  279.7 12.9 %collective-permute-start.6 = (bf16[1,128,256]{2,1,0:T(8,128)(2,1)S(1)}, bf16[1,128,256]{2,1,0:T(8,128)(2,1)S(1)}, u32[]{:S(2)}, u32[]{:S(2)}) collective-permute-start(bf16[1,128,256]{2,1,0:T(8,128)(2,1)S(1)} %slice.143), channel_id=1, source_target_pairs={{0,32},{32,64},{64,96},{96,128},{128,160},{160,192},{192,224},{224... | collective-permute-start | bytes 196616 | tf_op jit(solution)/shard_map/ppermute | solution.py:16
  281.5 11.1 %collective-permute-start.7 = (bf16[1,128,256]{2,1,0:T(8,128)(2,1)S(1)}, bf16[1,128,256]{2,1,0:T(8,128)(2,1)S(1)}, u32[]{:S(2)}, u32[]{:S(2)}) collective-permute-start(bf16[1,128,256]{2,1,0:T(8,128)(2,1)S(1)} %slice.145), channel_id=1, source_target_pairs={{32,0},{64,32},{96,64},{128,96},{160,128},{192,160},{224,192},{0,2... | collective-permute-start | bytes 196616 | tf_op jit(solution)/shard_map/ppermute | solution.py:18
  284.6 6.8 collective-permute-start.4
  (19 other events, 69.3 us)
Sparse Core Ops, SparseCore 0:
  202.8 213.8 reduce-scatter.7
  420.8 190.8 reduce-scatter.5
  615.5 199.1 reduce-scatter.3
where the time goes:
time: 851 us; the launch traced here: 850 us
  waiting for transfers between devices  522 us (61%)
  blocking collectives  138 us (16%)
  matrix products  74.1 us (9%)
  starting transfers between devices  54.8 us (6%)
  local copies, waits for them, and re-layouts  34.1 us (4%)
  between operations  14.2 us (2%)
  other arithmetic  11.7 us (1%)
    reduce_scatter x1, waiting for transfers between devices, body(): lax.psum_scatter(whole[0].astype(jnp.bfloat16), 'fsdp', scatter_dimension...  203 us
    reduce_scatter x1, waiting for transfers between devices, body(): lax.psum_scatter(whole[1].astype(jnp.bfloat16), 'fsdp', scatter_dimension...  195 us
    reduce_scatter x1, waiting for transfers between devices, body(): lax.psum_scatter(whole[2].astype(jnp.bfloat16), 'fsdp', scatter_dimension...  122 us
    all_gather x1, blocking collectives, body(): lax.all_gather(w_first, 'fsdp', axis=0, tiled=True)  40.3 us
    all_gather x1, blocking collectives, body(): lax.all_gather(w_second, 'fsdp', axis=0, tiled=True)  36 us
    all_gather x1, blocking collectives, body(): lax.all_gather(w_third, 'fsdp', axis=0, tiled=True)  35.4 us
    ppermute x6, starting transfers between devices, extended(): lax.ppermute(tail, axis, [(i, (i + 1) % count) for i in range(count)])  35.4 us
    dot_general x1, matrix products, forward_pass(): first_pre = jnp.dot(stacked, w_first, preferred_element_type=jnp.float32)  27.2 us
  transfers between devices with their start and end apart: 15, of which 4 were waited for; matrix products, arithmetic and copies ran while one was open for 6% of the time, Pallas kernels for 0%

commit v1 on v0

v1 whole, which is shorter than its diff:
```python
import jax
import jax.numpy as jnp
from jax import lax
from jax.experimental import pallas as pl
from jax.experimental.pallas import tpu as pltpu
from jax.sharding import PartitionSpec as P

BLOCK = 128
D = 256
NBD = 6
NH = 4
NEXT = NBD + NH
PAIRS = 16
NX, NY, NZ = 4, 4, 8
NZH = NZ // 2
UNITS = 5
CHUNK = 4
MESH = pl.DeviceIdType.MESH
F32, BF16 = jnp.float32, jnp.bfloat16


def place():
    a = lax.axis_index("dom")
    f = lax.axis_index("fsdp")
    return a, f, a // 2, lax.rem(a, 2), f // NZ, lax.rem(f, NZ)


def halo_peers(a, f):
    nd, nf = 2 * NX, NY * NZ
    return (
        (a, lax.rem(f + nf - 1, nf)),
        (a, lax.rem(f + 1, nf)),
        (lax.rem(a + nd - 1, nd), f),
        (lax.rem(a + 1, nd), f),
    )


def greet(peers):
    barrier = pltpu.get_barrier_semaphore()
    for peer in peers:
        pl.semaphore_signal(barrier, inc=1, device_id=peer, device_id_type=MESH)
    pl.semaphore_wait(barrier, len(peers))


def remote(src, dst, send, recv, peer):
    return pltpu.make_async_remote_copy(
        src_ref=src, dst_ref=dst, send_sem=send, recv_sem=recv,
        device_id=peer, device_id_type=MESH,
    )


def gather_kernel(
    sf, sd, w1, w2, w3, node, cot, wall, halo, lend,
    zs, zr, ys, yr, ss, sr, hs, hr,
):
    a, f, x, c, y, z = place()
    zh, zc = z // 2, lax.rem(z, 2)
    sib = (a + 1 - 2 * c, f)
    zpeers = [(a, y * NZ + lax.rem(z + d, NZ)) for d in range(1, NZ)]
    ypeers = [(a, lax.rem(y + d, NY) * NZ + z) for d in range(1, NY)]
    hpeers = halo_peers(a, f)

    for s in range(2):
        b = sf[s]
        lend[s, 0] = node[b]
        lend[s, 1] = cot[b]
        b = sd[s]
        lend[2 + s, 0] = node[b]
        lend[2 + s, 1] = cot[b]

    @pl.when(zc == c)
    def _():
        wall[y, zh, c, 0:3] = w1[...].astype(F32).reshape(3, 8, D).astype(BF16)
        wall[y, zh, c, 3] = w2[...]
        wall[y, zh, c, 4] = w3[...]

    greet(zpeers + ypeers + [sib] + list(hpeers))

    halos = [
        remote(lend.at[s], halo.at[s ^ 1], hs.at[s], hr.at[s ^ 1], hpeers[s])
        for s in range(NH)
    ]
    zcopies = [
        remote(wall.at[y, zh, c], wall.at[y, zh, c], zs.at[d], zr.at[zh], peer)
        for d, peer in enumerate(zpeers)
    ]

    @pl.when(zc == c)
    def _():
        for copy in zcopies:
            copy.start()

    halos[2].start()
    halos[3].start()

    for h in range(NZH):
        @pl.when(2 * h + c != z)
        def _():
            remote(
                wall.at[y, h, c], wall.at[y, h, c], zs.at[0], zr.at[h], sib
            ).wait_recv()

    def part(yy, cc):
        return wall.at[yy, :, cc]

    ycopies = [
        remote(part(y, c), part(y, c), ys.at[d], yr.at[y], peer)
        for d, peer in enumerate(ypeers)
    ]
    for copy in ycopies:
        copy.start()
    scopies = [remote(part(y, c), part(y, c), ss.at[0], sr.at[0], sib)]
    scopies[0].start()
    halos[0].start()
    halos[1].start()
    for d in range(1, NY):
        yy = lax.rem(y + d, NY)
        remote(part(yy, c), part(yy, c), ys.at[0], yr.at[yy], sib).wait_recv()
        copy = remote(part(yy, c), part(yy, c), ss.at[d], sr.at[d], sib)
        copy.start()
        scopies.append(copy)
    for d in range(NY):
        yy = lax.rem(y + d, NY)
        remote(part(yy, 1 - c), part(yy, 1 - c), ss.at[d], sr.at[d], sib).wait_recv()
    for s in range(NH):
        halos[s].wait_recv()

    @pl.when(zc == c)
    def _():
        for copy in zcopies:
            copy.wait_send()

    for copy in ycopies + scopies + halos:
        copy.wait_send()


def gather(sf, sd, w1, w2, w3, node, cot):
    smem = pl.BlockSpec(memory_space=pltpu.SMEM)
    vmem = pl.BlockSpec(memory_space=pltpu.VMEM)
    dma = pltpu.SemaphoreType.DMA
    return pl.pallas_call(
        gather_kernel,
        out_shape=(
            jax.ShapeDtypeStruct((NY, NZH, 2, UNITS, 8, D), BF16),
            jax.ShapeDtypeStruct((NH, 2, BLOCK, D), BF16),
        ),
        in_specs=[smem, smem] + [vmem] * 5,
        out_specs=(vmem, vmem),
        scratch_shapes=[
            pltpu.VMEM((NH, 2, BLOCK, D), BF16),
            dma((NZ - 1,)), dma((NZH,)), dma((NY - 1,)), dma((NY,)),
            dma((NY,)), dma((NY,)), dma((NH,)), dma((NH,)),
        ],
        compiler_params=pltpu.CompilerParams(
            collective_id=0, has_side_effects=True, vmem_limit_bytes=24 << 20
        ),
        name="gather",
    )(sf, sd, w1, w2, w3, node, cot)


def mm(p, q):
    return jnp.dot(p, q, preferred_element_type=F32)


def mm_t(p, q):
    return lax.dot_general(p, q, (((1,), (1,)), ((), ())), preferred_element_type=F32)


def t_mm(p, q):
    return lax.dot_general(p, q, (((0,), (0,)), ((), ())), preferred_element_type=F32)


def act_slope(half):
    up = 1.0 + jnp.tanh(half)
    act = half * up
    return act, up + act * (2.0 - up)


def compute_kernel(
    near, far, wall, halo, node, cot, edge,
    out_edge, state_part, grad_part, back, grads,
    w1, w1h, w2h, w3, w3h, left, right, ctab, tsum, ysum, a1, d1, gg, sg, dd, ef,
    acc_1, acc_2, acc_3,
):
    step = pl.program_id(0)

    @pl.when(step == 0)
    def _():
        packed = wall[...].astype(F32)
        first = packed[:, 0:3].reshape(3 * D, D)
        w1[...] = first.astype(BF16)
        w1h[...] = (0.5 * first).astype(BF16)
        w2h[...] = (0.5 * packed[:, 3].reshape(D, D)).astype(BF16)
        third = packed[:, 4].reshape(D, D)
        w3[...] = third.astype(BF16)
        w3h[...] = (0.5 * third).astype(BF16)
        own = node[...].reshape(NBD * BLOCK, D)
        lent = halo[:, 0].reshape(NH * BLOCK, D)
        for table, cols in ((left, 0), (right, D)):
            weight = w1h[cols:cols + D]
            table[0:NBD] = mm(own, weight).reshape(NBD, BLOCK, D)
            table[NBD:] = mm(lent, weight).reshape(NH, BLOCK, D)
        ctab[0:NBD] = cot[...]
        ctab[NBD:] = halo[:, 1]
        tsum[...] = jnp.zeros_like(tsum)
        ysum[...] = jnp.zeros_like(ysum)
        acc_1[...] = jnp.zeros_like(acc_1)
        acc_2[...] = jnp.zeros_like(acc_2)
        acc_3[...] = jnp.zeros_like(acc_3)

    pairs = [(near[step * CHUNK + j], far[step * CHUNK + j]) for j in range(CHUNK)]
    rows = [slice(j * BLOCK, (j + 1) * BLOCK) for j in range(CHUNK)]
    half = CHUNK * BLOCK
    mirror = [slice(half + j * BLOCK, half + (j + 1) * BLOCK) for j in range(CHUNK)]

    edge_part = mm(edge[...], w1h[2 * D:])
    for j, (n, t) in enumerate(pairs):
        gg[rows[j]] = (ctab[n].astype(F32) - ctab[t].astype(F32)).astype(BF16)
        for where, p, q in ((rows[j], n, t), (mirror[j], t, n)):
            act, slope = act_slope(left[p] + right[q] + edge_part[rows[j]])
            a1[where] = act.astype(BF16)
            d1[where] = slope
    second = mm(a1[...], w2h[...])
    back_3 = mm_t(gg[...], w3h[...])
    for j, (n, t) in enumerate(pairs):
        act_f, slope_f = act_slope(second[rows[j]])
        act_m, slope_m = act_slope(second[mirror[j]])
        diff = act_f.astype(BF16).astype(F32) - act_m.astype(BF16).astype(F32)
        dd[rows[j]] = diff.astype(BF16)
        tsum[n] = tsum[n] + diff
        tsum[t] = tsum[t] - diff
        sg[rows[j]] = (back_3[rows[j]] * slope_f).astype(BF16)
        sg[mirror[j]] = (-back_3[rows[j]] * slope_m).astype(BF16)
    first_back = mm_t(sg[...], w2h[...])
    for j, (n, t) in enumerate(pairs):
        part_f = (first_back[rows[j]] * d1[rows[j]]).astype(BF16).astype(F32)
        part_m = (first_back[mirror[j]] * d1[mirror[j]]).astype(BF16).astype(F32)
        ef[rows[j]] = (part_f + part_m).astype(BF16)
        ysum[0, n] = ysum[0, n] + part_f
        ysum[0, t] = ysum[0, t] + part_m
        ysum[1, n] = ysum[1, n] + part_m
        ysum[1, t] = ysum[1, t] + part_f
    out_edge[...] = mm_t(ef[...], w1[2 * D:]).astype(BF16)
    acc_3[...] += t_mm(dd[...], gg[...])
    acc_2[...] += t_mm(a1[...], sg[...])
    acc_1[2 * D:] += t_mm(edge[...], ef[...])

    @pl.when(step == PAIRS // CHUNK - 1)
    def _():
        own_rows = NBD * BLOCK
        flux = mm(tsum[...].astype(BF16).reshape(NEXT * BLOCK, D), w3[...])
        state_part[...] = node[...].astype(F32) + flux[:own_rows].reshape(NBD, BLOCK, D)
        back[:, 0] = flux[own_rows:].astype(BF16).reshape(NH, BLOCK, D)
        ya = ysum[0].astype(BF16).reshape(NEXT * BLOCK, D)
        yb = ysum[1].astype(BF16).reshape(NEXT * BLOCK, D)
        node_grad = mm_t(ya, w1[0:D]) + mm_t(yb, w1[D:2 * D])
        grad_part[...] = cot[...].astype(F32) + node_grad[:own_rows].reshape(NBD, BLOCK, D)
        back[:, 1] = node_grad[own_rows:].astype(BF16).reshape(NH, BLOCK, D)
        own = node[...].reshape(own_rows, D)
        lent = halo[:, 0].reshape(NH * BLOCK, D)
        acc_1[0:D] = t_mm(own, ya[:own_rows]) + t_mm(lent, ya[own_rows:])
        acc_1[D:2 * D] = t_mm(own, yb[:own_rows]) + t_mm(lent, yb[own_rows:])
        grads[:, 0:3] = acc_1[...].reshape(NY * NZ, 3, 8, D).astype(BF16)
        grads[:, 3] = acc_2[...].reshape(NY * NZ, 8, D).astype(BF16)
        grads[:, 4] = acc_3[...].reshape(NY * NZ, 8, D).astype(BF16)


def compute(near, far, wall, halo, node, cot, edge):
    smem = pl.BlockSpec(memory_space=pltpu.SMEM)
    vmem = pl.BlockSpec(memory_space=pltpu.VMEM)
    chunk = pl.BlockSpec((CHUNK * BLOCK, D), lambda i: (i, 0))
    rows = CHUNK * BLOCK
    table = pltpu.VMEM((NEXT, BLOCK, D), F32)
    return pl.pallas_call(
        compute_kernel,
        grid=(PAIRS // CHUNK,),
        out_shape=(
            jax.ShapeDtypeStruct(edge.shape, BF16),
            jax.ShapeDtypeStruct((NBD, BLOCK, D), F32),
            jax.ShapeDtypeStruct((NBD, BLOCK, D), F32),
            jax.ShapeDtypeStruct((NH, 2, BLOCK, D), BF16),
            jax.ShapeDtypeStruct((NY * NZ, UNITS, 8, D), BF16),
        ),
        in_specs=[smem, smem] + [vmem] * 4 + [chunk],
        out_specs=(chunk, vmem, vmem, vmem, vmem),
        scratch_shapes=[
            pltpu.VMEM((3 * D, D), BF16), pltpu.VMEM((3 * D, D), BF16),
            pltpu.VMEM((D, D), BF16), pltpu.VMEM((D, D), BF16), pltpu.VMEM((D, D), BF16),
            table, table, pltpu.VMEM((NEXT, BLOCK, D), BF16),
            table, pltpu.VMEM((2, NEXT, BLOCK, D), F32),
            pltpu.VMEM((2 * rows, D), BF16), pltpu.VMEM((2 * rows, D), F32),
            pltpu.VMEM((rows, D), BF16), pltpu.VMEM((2 * rows, D), BF16),
            pltpu.VMEM((rows, D), BF16), pltpu.VMEM((rows, D), BF16),
            pltpu.VMEM((3 * D, D), F32), pltpu.VMEM((D, D), F32), pltpu.VMEM((D, D), F32),
        ],
        compiler_params=pltpu.CompilerParams(vmem_limit_bytes=48 << 20),
        name="layer",
    )(near, far, wall, halo, node, cot, edge)


def reduce_kernel(
    sf, sd, grads, state_part, grad_part, back, new_state, grad_state, total,
    got, sibbuf, q, xbuf, r, ybuf, t, zbuf, fin, finbuf,
    hs, hr, ss, sr, xs, xr, ys, yr, zs, zr, fs, fr,
):
    a, f, x, c, y, z = place()
    sib = (a + 1 - 2 * c, f)
    xpeers = [(2 * lax.rem(x + d, NX) + c, f) for d in range(1, NX)]
    ypeers = [(a, lax.rem(y + d, NY) * NZ + z) for d in range(1, NY)]
    zpeers = [(a, y * NZ + lax.rem(z + d, NZ)) for d in range(1, NZ)]
    dpeers = [(lax.rem(a + d, 2 * NX), f) for d in range(1, 2 * NX)]
    hpeers = halo_peers(a, f)
    greet(dpeers + ypeers + zpeers + list(hpeers))

    copy_s = remote(grads.at[:, :, 1 - c], sibbuf, ss, sr, sib)
    copy_s.start()
    halos = [
        remote(back.at[s], got.at[s ^ 1], hs.at[s], hr.at[s ^ 1], hpeers[s])
        for s in range(NH)
    ]
    for copy in halos:
        copy.start()

    copy_s.wait_recv()
    q[...] = (grads[:, :, c].astype(F32) + sibbuf[...].astype(F32)).astype(BF16)
    xcopies = []
    for d, peer in enumerate(xpeers):
        copy = remote(q.at[:, lax.rem(x + d + 1, NX)], xbuf.at[d], xs.at[d], xr.at[d], peer)
        copy.start()
        xcopies.append(copy)

    for copy in halos:
        copy.wait_recv()
    owner = (sf[0], sf[1], sd[0], sd[1])
    for b in range(NBD):
        for k, (part, out) in enumerate(((state_part, new_state), (grad_part, grad_state))):
            value = part[b]
            for s in range(NH):
                value = value + jnp.where(owner[s] == b, got[s, k].astype(F32), 0.0)
            out[b] = value.astype(BF16)

    value = q[:, x].astype(F32)
    for d, copy in enumerate(xcopies):
        copy.wait_recv()
        value = value + xbuf[d].astype(F32)
    r[...] = value.astype(BF16)
    ycopies = []
    for d, peer in enumerate(ypeers):
        copy = remote(r.at[lax.rem(y + d + 1, NY)], ybuf.at[d], ys.at[d], yr.at[d], peer)
        copy.start()
        ycopies.append(copy)
    value = r[y].astype(F32)
    for d, copy in enumerate(ycopies):
        copy.wait_recv()
        value = value + ybuf[d].astype(F32)
    t[...] = value.astype(BF16)

    copy_z = remote(t, zbuf.at[z], zs, zr.at[z], (a, y * NZ + a))
    fcopies = [
        remote(fin, finbuf, fs.at[d], fr, peer) for d, peer in enumerate(dpeers)
    ]

    @pl.when(z != a)
    def _():
        copy_z.start()
        remote(fin, finbuf, fs.at[0], fr, sib).wait_recv()
        total[...] = finbuf[...].astype(F32)

    @pl.when(z == a)
    def _():
        acc = t[...].astype(F32)
        for d in range(1, NZ):
            zz = lax.rem(z + d, NZ)
            remote(t, zbuf.at[zz], zs, zr.at[zz], sib).wait_recv()
            acc = acc + zbuf[zz].astype(F32)
        fin[...] = acc.astype(BF16)
        for copy in fcopies:
            copy.start()
        total[...] = fin[...].astype(F32)

    copy_s.wait_send()
    for copy in halos + xcopies + ycopies:
        copy.wait_send()

    @pl.when(z != a)
    def _():
        copy_z.wait_send()

    @pl.when(z == a)
    def _():
        for copy in fcopies:
            copy.wait_send()


def reduce(sf, sd, grads, state_part, grad_part, back):
    smem = pl.BlockSpec(memory_space=pltpu.SMEM)
    vmem = pl.BlockSpec(memory_space=pltpu.VMEM)
    dma = pltpu.SemaphoreType.DMA
    shard = (UNITS, 8, D)
    return pl.pallas_call(
        reduce_kernel,
        out_shape=(
            jax.ShapeDtypeStruct((NBD, BLOCK, D), BF16),
            jax.ShapeDtypeStruct((NBD, BLOCK, D), BF16),
            jax.ShapeDtypeStruct(shard, F32),
        ),
        in_specs=[smem, smem] + [vmem] * 4,
        out_specs=(vmem, vmem, vmem),
        scratch_shapes=[
            pltpu.VMEM((NH, 2, BLOCK, D), BF16),
            pltpu.VMEM((NY, NZH, *shard), BF16), pltpu.VMEM((NY, NZH, *shard), BF16),
            pltpu.VMEM((NX - 1, NY, *shard), BF16), pltpu.VMEM((NY, *shard), BF16),
            pltpu.VMEM((NY - 1, *shard), BF16), pltpu.VMEM(shard, BF16),
            pltpu.VMEM((NZ, *shard), BF16), pltpu.VMEM(shard, BF16), pltpu.VMEM(shard, BF16),
            dma((NH,)), dma((NH,)), dma, dma,
            dma((NX - 1,)), dma((NX - 1,)), dma((NY - 1,)), dma((NY - 1,)),
            dma, dma((NZ,)), dma((2 * NX - 1,)), dma,
        ],
        compiler_params=pltpu.CompilerParams(
            collective_id=1, has_side_effects=True, vmem_limit_bytes=32 << 20
        ),
        name="reduce",
    )(sf, sd, grads, state_part, grad_part, back)


def body(node_state, edge_state, cotangent, w_first, w_second, w_third,
         pair_near, pair_far, send_fsdp, send_dom):
    node = node_state.reshape(NBD, BLOCK, D)
    cot = cotangent.reshape(NBD, BLOCK, D)
    sf = send_fsdp.reshape(2)
    sd = send_dom.reshape(2)
    wall, halo = gather(sf, sd, w_first, w_second, w_third, node, cot)
    grad_edges, state_part, grad_part, back, grads = compute(
        pair_near, pair_far, wall.reshape(NY * NZ, UNITS, 8, D), halo, node, cot, edge_state
    )
    new_state, grad_state, total = reduce(
        sf, sd, grads.reshape(NY, NZH, 2, UNITS, 8, D), state_part, grad_part, back
    )
    return (
        new_state.reshape(NBD * BLOCK, D),
        grad_state.reshape(NBD * BLOCK, D),
        grad_edges,
        total[0:3].reshape(24, D),
        total[3],
        total[4],
    )


def solution(mesh):
    cells = P(("dom", "fsdp"), None)
    rows = P("fsdp", None)
    flat = P(("dom", "fsdp"))
    lists = P(("dom", "fsdp"), None, None)
    return jax.shard_map(
        body,
        mesh=mesh,
        in_specs=(cells, cells, cells, rows, rows, rows, flat, flat, lists, lists),
        out_specs=(cells, cells, cells, rows, rows, rows),
        check_vma=False,
    )
```

time: 851 us -> 66.4 us (0.08)
  waiting for transfers between devices: 522 us -> 0 us
  blocking collectives: 138 us -> 0 us
  matrix products: 74.1 us -> 0 us
  Pallas kernels: 0 us -> 56 us
  starting transfers between devices: 54.8 us -> 0 us
  local copies, waits for them, and re-layouts: 34.1 us -> 8.63 us
  between operations: 14.2 us -> 0.72 us
  other arithmetic: 11.7 us -> 0 us
    reduce_scatter x3 -> x0, waiting for transfers between devices: 520 us -> none  [the longest x1 203 us: body(): lax.psum_scatter(whole[0].astype(jnp.bfloat16), 'fsdp', scatter_dimension...]
    all_gather x3 -> x0, blocking collectives: 112 us -> none  [the longest x1 40.3 us: body(): lax.all_gather(w_first, 'fsdp', axis=0, tiled=True)]
    dot_general x22 -> x0, matrix products: 74.1 us -> none  [the longest x1 27.2 us: forward_pass(): first_pre = jnp.dot(stacked, w_first, preferred_element_type=jnp.float32)]
    pallas_call x0 -> x3, Pallas kernels: none -> 56 us  [the longest x1 23.8 us: gather(): pl.pallas_call(gather_kernel, out_shape=(jax.ShapeDtypeStruct((NY, NZH, 2...]
    ppermute x12 -> x0, starting transfers between devices: 54.7 us -> none  [the longest x6 35.4 us: extended(): lax.ppermute(tail, axis, [(i, (i + 1) % count) for i in range(count)])]
    psum x1 -> x0, blocking collectives: 26.6 us -> none  [body(): lax.psum(grads[0].astype(jnp.bfloat16), 'dom').astype(jnp.float32)]
    gather x8 -> x0, local copies, waits for them, and re-layouts: 10.6 us -> none  [the longest x2 3.1 us: body(): lend_fsdp = jnp.stack([node_blocks[ids_fsdp], cot_blocks[ids_fsdp]], 1)]
    slice x12 -> x0, local copies, waits for them, and re-layouts: 9.88 us -> none  [the longest x6 5.18 us: extended(): lax.slice_in_dim(cells, cells.shape[dim] - width, cells.shape[dim], axis=...]
  transfers between devices with their start and end apart: 15 -> 0, of which waited for: 4 -> 0; matrix products, arithmetic and copies ran while one was open for 6% -> 0% of each run, Pallas kernels for 0% -> 0%
where the time goes in v1:
time: 66.4 us; the launch traced here: 65.3 us
  Pallas kernels  56 us (84%)
  local copies, waits for them, and re-layouts  8.63 us (13%)
  between operations  0.72 us (1%)
    pallas_call x1, Pallas kernels, gather(): pl.pallas_call(gather_kernel, out_shape=(jax.ShapeDtypeStruct((NY, NZH, 2...  23.8 us
    pallas_call x1, Pallas kernels, reduce(): pl.pallas_call(reduce_kernel, out_shape=(jax.ShapeDtypeStruct((NBD, BLOCK...  22 us
    pallas_call x1, Pallas kernels, compute(): pl.pallas_call(compute_kernel, grid=(PAIRS // CHUNK,), out_shape=(jax.Sha...  10.2 us
    unnamed x26, local copies, waits for them, and re-layouts  7.41 us

profile of v1, /device:TPU:1, one launch (start us, length us, event | category | flops | bytes accessed | tf_op | source)
XLA Modules:
  0.0 65.3 jit_solution(13710950190978454958)
XLA Ops:
  0.6 0.0 copy-start.6
  0.6 0.0 copy-start.8
  0.7 0.0 copy-start.9
  0.7 0.7 %copy-done.6 = bf16[8,256]{1,0:T(8,128)(2,1)S(1)} copy-done((bf16[8,256]{1,0:T(8,128)(2,1)S(1)}, bf16[8,256]{1,0:T(8,128)(2,1)}, u32[]{:S(2)}) %copy-start.6) | copy-done | bytes 4120
  1.3 0.0 copy-done.8
  1.3 0.0 copy-done.9
  1.3 1.0 %copy-done = bf16[768,256]{1,0:T(8,128)(2,1)S(1)} copy-done((bf16[768,256]{1,0:T(8,128)(2,1)S(1)}, bf16[768,256]{1,0:T(8,128)(2,1)}, u32[]{:S(2)}) %copy-start) | copy-done | bytes 393240
  2.3 1.0 %copy-done.2 = bf16[768,256]{1,0:T(8,128)(2,1)S(1)} copy-done((bf16[768,256]{1,0:T(8,128)(2,1)S(1)}, bf16[768,256]{1,0:T(8,128)(2,1)}, u32[]{:S(2)}) %copy-start.2) | copy-done | bytes 393240
  3.3 0.7 %copy-done.5 = bf16[24,256]{1,0:T(8,128)(2,1)S(1)} copy-done((bf16[24,256]{1,0:T(8,128)(2,1)S(1)}, bf16[24,256]{1,0:T(8,128)(2,1)}, u32[]{:S(2)}) %copy-start.5) | copy-done | bytes 12312
  4.0 0.7 %copy-done.7 = bf16[8,256]{1,0:T(8,128)(2,1)S(1)} copy-done((bf16[8,256]{1,0:T(8,128)(2,1)S(1)}, bf16[8,256]{1,0:T(8,128)(2,1)}, u32[]{:S(2)}) %copy-start.7) | copy-done | bytes 4120
  4.7 23.8 %gather.1 = (bf16[4,4,2,5,8,256]{5,4,3,2,1,0:T(8,128)(2,1)S(1)}, bf16[4,2,128,256]{3,2,1,0:T(8,128)(2,1)S(1)}) custom-call(s32[2]{0:T(128)S(1)} %bitcast.22, s32[2]{0:T(128)S(1)} %bitcast.24, bf16[24,256]{1,0:T(8,128)(2,1)S(1)} %copy-done.5, bf16[8,256]{1,0:T(8,128)(2,1)S(1)} %copy-done.6, bf16[8,256]{1,0:T(8,128)(2,1)S(1)} %copy-done.7, ...), custom_call_target="tpu_custom_call" | custom-call | tf_op jit(solution)/shard_map/gather/pallas_call | solution.py:141
  28.5 0.0 copy-start.10
  28.5 0.0 copy-start.11
  28.5 0.0 copy-done.1
  28.5 0.0 copy-done.3
  28.5 0.6 copy-done.10
  29.1 0.0 copy-done.11
  29.2 1.2 %copy-done.4 = bf16[2048,256]{1,0:T(8,128)(2,1)S(1)} copy-done((bf16[2048,256]{1,0:T(8,128)(2,1)S(1)}, bf16[2048,256]{1,0:T(8,128)(2,1)}, u32[]{:S(2)}) %copy-start.4) | copy-done | bytes 1048600
  30.4 10.2 %layer.1 = (bf16[2048,256]{1,0:T(8,128)(2,1)}, f32[6,128,256]{2,1,0:T(8,128)S(1)}, f32[6,128,256]{2,1,0:T(8,128)S(1)}, bf16[4,2,128,256]{3,2,1,0:T(8,128)(2,1)S(1)}, bf16[32,5,8,256]{3,2,1,0:T(8,128)(2,1)S(1)}) custom-call(s32[16]{0:T(128)S(1)} %copy-done.10, s32[16]{0:T(128)S(1)} %copy-done.11, bf16[32,5,8,256]{3,2,1,0:T(8,128)(2,1)S(1)} %bitcast.19, ...), custom_call_target="tpu_custom_call" | custom-call | tf_op jit(solution)/shard_map/layer/pallas_call | solution.py:274
  40.6 22.0 %reduce.1 = (bf16[6,128,256]{2,1,0:T(8,128)(2,1)S(1)}, bf16[6,128,256]{2,1,0:T(8,128)(2,1)S(1)}, f32[5,8,256]{2,1,0:T(8,128)S(1)}) custom-call(s32[2]{0:T(128)S(1)} %bitcast.23, s32[2]{0:T(128)S(1)} %bitcast.25, bf16[4,4,2,5,8,256]{5,4,3,2,1,0:T(8,128)(2,1)S(1)} %bitcast.18, f32[6,128,256]{2,1,0:T(8,128)S(1)} %get-tuple-element.19.state_part, ...), custom_call_target="tpu_custom_call" | custom-call | tf_op jit(solution)/shard_map/reduce/pallas_call | solution.py:400
  62.6 0.6 slice_bitcast_fusion.1
  63.2 0.6 slice_bitcast_fusion
  63.8 0.7 %copy.18 = bf16[768,256]{1,0:T(8,128)(2,1)} copy(bf16[768,256]{1,0:T(8,128)(2,1)S(1)} %bitcast.21) | data formatting | bytes 786432
  64.6 0.7 %copy.19 = bf16[768,256]{1,0:T(8,128)(2,1)} copy(bf16[768,256]{1,0:T(8,128)(2,1)S(1)} %bitcast.20) | data formatting | bytes 786432
  (7 shorter events, 0.0 us)
Async XLA Ops:
  0.6 0.7 %copy-start.6 = (bf16[8,256]{1,0:T(8,128)(2,1)S(1)}, bf16[8,256]{1,0:T(8,128)(2,1)}, u32[]{:S(2)}) copy-start(bf16[8,256]{1,0:T(8,128)(2,1)} %w2.1) | copy-start | bytes 12292
  0.6 0.7 %copy-start.8 = (s32[1,2,1]{1,2,0:T(1,128)S(1)}, s32[1,2,1]{1,2,0:T(1,128)}, u32[]{:S(2)}) copy-start(s32[1,2,1]{1,2,0:T(1,128)} %param.18) | copy-start | bytes 28
  0.7 0.7 %copy-start.9 = (s32[1,2,1]{1,2,0:T(1,128)S(1)}, s32[1,2,1]{1,2,0:T(1,128)}, u32[]{:S(2)}) copy-start(s32[1,2,1]{1,2,0:T(1,128)} %param.19) | copy-start | bytes 28
  1.3 1.0 %copy-start = (bf16[768,256]{1,0:T(8,128)(2,1)S(1)}, bf16[768,256]{1,0:T(8,128)(2,1)}, u32[]{:S(2)}) copy-start(bf16[768,256]{1,0:T(8,128)(2,1)} %param.10) | copy-start | bytes 1179652
  2.3 1.0 %copy-start.2 = (bf16[768,256]{1,0:T(8,128)(2,1)S(1)}, bf16[768,256]{1,0:T(8,128)(2,1)}, u32[]{:S(2)}) copy-start(bf16[768,256]{1,0:T(8,128)(2,1)} %param.12) | copy-start | bytes 1179652
  3.3 0.7 %copy-start.5 = (bf16[24,256]{1,0:T(8,128)(2,1)S(1)}, bf16[24,256]{1,0:T(8,128)(2,1)}, u32[]{:S(2)}) copy-start(bf16[24,256]{1,0:T(8,128)(2,1)} %w1.1) | copy-start | bytes 36868
  4.0 0.7 %copy-start.7 = (bf16[8,256]{1,0:T(8,128)(2,1)S(1)}, bf16[8,256]{1,0:T(8,128)(2,1)}, u32[]{:S(2)}) copy-start(bf16[8,256]{1,0:T(8,128)(2,1)} %w3.1) | copy-start | bytes 12292
  4.7 23.8 %copy-start.1 = (bf16[768,256]{1,0:T(8,128)(2,1)S(1)}, bf16[768,256]{1,0:T(8,128)(2,1)}, u32[]{:S(2)}) copy-start(bf16[768,256]{1,0:T(8,128)(2,1)} %param.10) | copy-start | bytes 1179652
  4.7 23.8 %copy-start.3 = (bf16[768,256]{1,0:T(8,128)(2,1)S(1)}, bf16[768,256]{1,0:T(8,128)(2,1)}, u32[]{:S(2)}) copy-start(bf16[768,256]{1,0:T(8,128)(2,1)} %param.12) | copy-start | bytes 1179652
  28.5 0.7 %copy-start.10 = (s32[16]{0:T(128)S(1)}, s32[16]{0:T(128)}, u32[]{:S(2)}) copy-start(s32[16]{0:T(128)} %near.1) | copy-start | bytes 196
  28.5 0.7 %copy-start.11 = (s32[16]{0:T(128)S(1)}, s32[16]{0:T(128)}, u32[]{:S(2)}) copy-start(s32[16]{0:T(128)} %far.1) | copy-start | bytes 196
  29.2 1.2 %copy-start.4 = (bf16[2048,256]{1,0:T(8,128)(2,1)S(1)}, bf16[2048,256]{1,0:T(8,128)(2,1)}, u32[]{:S(2)}) copy-start(bf16[2048,256]{1,0:T(8,128)(2,1)} %edge.1) | copy-start | bytes 3145732

commit v2 on v1

v2 whole, which is shorter than its diff:
```python
import jax
import jax.numpy as jnp
from jax import lax
from jax.experimental import pallas as pl
from jax.experimental.pallas import tpu as pltpu
from jax.sharding import PartitionSpec as P

BLOCK = 128
D = 256
NBD = 6
NH = 4
NEXT = NBD + NH
PAIRS = 16
NX, NY, NZ = 4, 4, 8
NZH = NZ // 2
UNITS = 5
CHUNK = 4
UNROLL = False
VMEM_MIB = 58
MESH = pl.DeviceIdType.MESH
F32, BF16 = jnp.float32, jnp.bfloat16


def place():
    a = lax.axis_index("dom")
    f = lax.axis_index("fsdp")
    return a, f, a // 2, lax.rem(a, 2), f // NZ, lax.rem(f, NZ)


def halo_peers(a, f):
    nd, nf = 2 * NX, NY * NZ
    return (
        (a, lax.rem(f + nf - 1, nf)),
        (a, lax.rem(f + 1, nf)),
        (lax.rem(a + nd - 1, nd), f),
        (lax.rem(a + 1, nd), f),
    )


def signal_all(peers):
    barrier = pltpu.get_barrier_semaphore()
    for peer in peers:
        pl.semaphore_signal(barrier, inc=1, device_id=peer, device_id_type=MESH)


def wait_all(count):
    pl.semaphore_wait(pltpu.get_barrier_semaphore(), count)


def remote(src, dst, send, recv, peer):
    return pltpu.make_async_remote_copy(
        src_ref=src, dst_ref=dst, send_sem=send, recv_sem=recv,
        device_id=peer, device_id_type=MESH,
    )


def mm(p, q):
    return jnp.dot(p, q, preferred_element_type=F32)


def mm_t(p, q):
    return lax.dot_general(p, q, (((1,), (1,)), ((), ())), preferred_element_type=F32)


def t_mm(p, q):
    return lax.dot_general(p, q, (((0,), (0,)), ((), ())), preferred_element_type=F32)


def act_slope(half):
    up = 1.0 + jnp.tanh(half)
    act = half * up
    return act, up + act * (2.0 - up)


def layer_kernel(
    near_hbm, far_hbm, sf_hbm, sd_hbm, w1_hbm, w2_hbm, w3_hbm, node_hbm, cot_hbm, edge_hbm,
    state_out, grad_out, edge_out, total_out,
    near, far, sf, sd, chain, last, w1s, w2s, w3s, node, cot, edge, lend, wall, halo,
    w1, w1h, w2h, w3, w3h, left, right, ctab, tsum, ysum, a1, d1, gg, sg, dd, ef,
    first, grads, back, state_part, grad_part,
    got, sibbuf, q, xbuf, r, ybuf, t, zbuf, fin, finbuf, new_state, grad_state, ge, total,
    os, ls, zs, zr, ys, yr, ss, sr, hs, hr, bs, br, s0, r0, xs, xr, y2s, y2r, z2s, z2r, fs, fr,
):
    a, f, x, c, y, z = place()
    zh, zc = z // 2, lax.rem(z, 2)
    sib = (a + 1 - 2 * c, f)
    xpeers = [(2 * lax.rem(x + d, NX) + c, f) for d in range(1, NX)]
    ypeers = [(a, lax.rem(y + d, NY) * NZ + z) for d in range(1, NY)]
    zpeers = [(a, y * NZ + lax.rem(z + d, NZ)) for d in range(1, NZ)]
    dpeers = [(lax.rem(a + d, 2 * NX), f) for d in range(1, 2 * NX)]
    hpeers = halo_peers(a, f)
    everyone = zpeers + ypeers + dpeers + list(hpeers)
    signal_all(everyone)

    loads = [
        pltpu.make_async_copy(src, dst, ls.at[i])
        for i, (src, dst) in enumerate((
            (w1_hbm, w1s), (w2_hbm, w2s), (w3_hbm, w3s), (sf_hbm, sf), (sd_hbm, sd),
            (node_hbm, node), (cot_hbm, cot), (near_hbm, near), (far_hbm, far), (edge_hbm, edge),
        ))
    ]
    for copy in loads:
        copy.start()
    for copy in loads[:3]:
        copy.wait()

    @pl.when(zc == c)
    def _():
        wall[y, zh, c, 0:3] = w1s[...].astype(F32).reshape(3, 8, D).astype(BF16)
        wall[y, zh, c, 3] = w2s[...]
        wall[y, zh, c, 4] = w3s[...]

    for copy in loads[3:7]:
        copy.wait()
    for s in range(2):
        b = sf[s]
        lend[s, 0] = node[b]
        lend[s, 1] = cot[b]
        b = sd[s]
        lend[2 + s, 0] = node[b]
        lend[2 + s, 1] = cot[b]
    wait_all(len(everyone))

    halos = [
        remote(lend.at[s], halo.at[s ^ 1], hs.at[s], hr.at[s ^ 1], hpeers[s])
        for s in range(NH)
    ]
    zcopies = [
        remote(wall.at[y, zh, c], wall.at[y, zh, c], zs.at[d], zr.at[zh], zpeers[d])
        for d in (3, 2, 4, 1, 5, 0, 6)
    ]

    @pl.when(zc == c)
    def _():
        for copy in zcopies:
            copy.start()

    halos[2].start()
    halos[3].start()

    loads[7].wait()
    loads[8].wait()
    keys = [(near, far)[h % 2][h // 2] for h in range(2 * PAIRS)]

    def link(h, carry):
        p = h // 2
        key = jnp.where(lax.rem(h, 2) == 0, near[p], far[p])
        before = jnp.int32(2 * PAIRS)
        for g in range(2 * PAIRS):
            before = jnp.where((keys[g] == key) & (g < h), g, before)
        chain[h] = before
        return carry

    lax.fori_loop(0, 2 * PAIRS, link, 0)

    def end(b, carry):
        where = jnp.int32(2 * PAIRS)
        for g in range(2 * PAIRS):
            where = jnp.where(keys[g] == b, g, where)
        last[b] = where
        return carry

    lax.fori_loop(0, NEXT, end, 0)

    sent = []

    def pass_on(yy, h, slot, along_y):
        part = wall.at[yy, h, c]
        if along_y:
            for d, peer in enumerate(ypeers):
                copy = remote(part, part, ys.at[slot, d], yr.at[y, h], peer)
                copy.start()
                sent.append(copy)
        copy = remote(part, part, ss.at[slot], sr.at[yy, h], sib)
        copy.start()
        sent.append(copy)

    for i, d in enumerate((0, 1, 3, 2)):
        h = lax.rem(zh + d, NZH)

        @pl.when(2 * h + c != z)
        def _():
            part = wall.at[y, h, c]
            remote(part, part, zs.at[0], zr.at[h], sib).wait_recv()

        pass_on(y, h, i, True)
    halos[0].start()
    halos[1].start()

    tsum[2 * PAIRS] = jnp.zeros((BLOCK, D), F32)
    ysum[0, 2 * PAIRS] = jnp.zeros((BLOCK, D), F32)
    ysum[1, 2 * PAIRS] = jnp.zeros((BLOCK, D), F32)
    ctab[0:NBD] = cot[...]

    for i, d in enumerate((0, 1, 3, 2)):
        h = lax.rem(zh + d, NZH)
        for e in (1, 3, 2):
            yy = lax.rem(y + e, NY)
            part = wall.at[yy, h, c]
            remote(part, part, ys.at[0, 0], yr.at[yy, h], sib).wait_recv()
            pass_on(yy, h, 4 * e + i, False)
    for s in range(NH):
        halos[s].wait_recv()
    loads[9].wait()
    rows = CHUNK * BLOCK
    direct = [slice(j * BLOCK, (j + 1) * BLOCK) for j in range(CHUNK)]
    mirror = [slice(rows + j * BLOCK, rows + (j + 1) * BLOCK) for j in range(CHUNK)]
    own_rows = NBD * BLOCK
    ctab[NBD:] = halo[:, 1]
    for yy in range(NY):
        for h in range(NZH):
            part = wall.at[yy, h, 1 - c]
            remote(part, part, ss.at[0], sr.at[yy, h], sib).wait_recv()

    packed = wall[...].reshape(NY * NZ, UNITS, 8, D).astype(F32)
    flat = packed[:, 0:3].reshape(3 * D, D)
    w1[...] = flat.astype(BF16)
    w1h[...] = (0.5 * flat).astype(BF16)
    w2h[...] = (0.5 * packed[:, 3].reshape(D, D)).astype(BF16)
    third = packed[:, 4].reshape(D, D)
    w3[...] = third.astype(BF16)
    w3h[...] = (0.5 * third).astype(BF16)
    own = node[...].reshape(own_rows, D)
    lent = halo[:, 0].reshape(NH * BLOCK, D)
    for table, cols in ((left, 0), (right, D)):
        weight = w1h[cols:cols + D]
        table[0:NBD] = mm(own, weight).reshape(NBD, BLOCK, D)
        table[NBD:] = mm(lent, weight).reshape(NH, BLOCK, D)

    def chunk(i, carry):
        pairs = [i * CHUNK + j for j in range(CHUNK)]
        ends = [(near[p], far[p]) for p in pairs]
        links = [(2 * p, chain[2 * p], chain[2 * p + 1]) for p in pairs]
        span = pl.ds(pl.multiple_of(i * rows, rows), rows)
        edge_part = mm(edge[span], w1h[2 * D:])
        for j, (n, m) in enumerate(ends):
            gg[i, direct[j]] = (ctab[n].astype(F32) - ctab[m].astype(F32)).astype(BF16)
            for where, p, k in ((direct[j], n, m), (mirror[j], m, n)):
                act, slope = act_slope(left[p] + right[k] + edge_part[direct[j]])
                a1[i, where] = act.astype(BF16)
                d1[where] = slope
        second = mm(a1[i], w2h[...])
        back_3 = mm_t(gg[i], w3h[...])
        for j, (h, before_n, before_m) in enumerate(links):
            act_f, slope_f = act_slope(second[direct[j]])
            act_m, slope_m = act_slope(second[mirror[j]])
            diff = act_f.astype(BF16).astype(F32) - act_m.astype(BF16).astype(F32)
            dd[i, direct[j]] = diff.astype(BF16)
            tsum[h] = tsum[before_n] + diff
            tsum[h + 1] = tsum[before_m] - diff
            sg[i, direct[j]] = (back_3[direct[j]] * slope_f).astype(BF16)
            sg[i, mirror[j]] = (-back_3[direct[j]] * slope_m).astype(BF16)
        first_back = mm_t(sg[i], w2h[...])
        for j, (h, before_n, before_m) in enumerate(links):
            part_f = (first_back[direct[j]] * d1[direct[j]]).astype(BF16).astype(F32)
            part_m = (first_back[mirror[j]] * d1[mirror[j]]).astype(BF16).astype(F32)
            ef[i, direct[j]] = (part_f + part_m).astype(BF16)
            ysum[0, h] = ysum[0, before_n] + part_f
            ysum[0, h + 1] = ysum[0, before_m] + part_m
            ysum[1, h] = ysum[1, before_n] + part_m
            ysum[1, h + 1] = ysum[1, before_m] + part_f
        ge[span] = mm_t(ef[i], w1[2 * D:]).astype(BF16)
        return carry

    lax.fori_loop(0, PAIRS // CHUNK, chunk, 0, unroll=UNROLL)
    stores = [
        pltpu.make_async_copy(src, dst, os.at[i])
        for i, (src, dst) in enumerate((
            (ge, edge_out), (new_state, state_out), (grad_state, grad_out), (total, total_out),
        ))
    ]
    stores[0].start()

    ends = [last[b] for b in range(NEXT)]

    def gathered(pick):
        return jnp.concatenate([pick(h).astype(BF16) for h in ends], 0)

    ts = gathered(lambda h: tsum[h])
    ya = gathered(lambda h: ysum[0, h])
    yb = gathered(lambda h: ysum[1, h])
    wa, wb = w1[0:D], w1[D:2 * D]

    lent_flux = mm(ts[own_rows:], w3[...])
    lent_grad = mm_t(ya[own_rows:], wa) + mm_t(yb[own_rows:], wb)
    back[:, 0] = lent_flux.astype(BF16).reshape(NH, BLOCK, D)
    back[:, 1] = lent_grad.astype(BF16).reshape(NH, BLOCK, D)
    backs = [
        remote(back.at[s], got.at[s ^ 1], bs.at[s], br.at[s ^ 1], hpeers[s])
        for s in range(NH)
    ]
    for copy in backs:
        copy.start()

    def whole(ref):
        return ref[...].reshape(-1, D)

    pieces = (slice(3, 5), slice(0, 3))

    def to_sibling(k):
        copy = remote(grads.at[:, :, 1 - c, pieces[k]], sibbuf.at[:, :, pieces[k]], s0.at[k], r0.at[k], sib)
        copy.start()
        return copy

    grads[:, :, :, 3] = t_mm(whole(a1), whole(sg)).reshape(NY, NZH, 2, 8, D).astype(BF16)
    grads[:, :, :, 4] = t_mm(whole(dd), whole(gg)).reshape(NY, NZH, 2, 8, D).astype(BF16)
    cores = [to_sibling(0)]
    first[0:D] = t_mm(own, ya[:own_rows]) + t_mm(lent, ya[own_rows:])
    first[D:2 * D] = t_mm(own, yb[:own_rows]) + t_mm(lent, yb[own_rows:])
    first[2 * D:] = t_mm(edge[...], whole(ef))
    grads[:, :, :, 0:3] = first[...].reshape(NY, NZH, 2, 3, 8, D).astype(BF16)
    cores.append(to_sibling(1))

    xcopies = []
    for k, piece in enumerate(pieces):
        if k:
            flux = mm(ts[:own_rows], w3[...]).reshape(NBD, BLOCK, D)
            state_part[...] = node[...].astype(F32) + flux
        cores[k].wait_recv()
        q[:, :, piece] = (grads[:, :, c, piece].astype(F32) + sibbuf[:, :, piece].astype(F32)).astype(BF16)
        for d, peer in enumerate(xpeers):
            xx = lax.rem(x + d + 1, NX)
            copy = remote(q.at[:, xx, piece], xbuf.at[d, :, piece], xs.at[k, d], xr.at[k, d], peer)
            copy.start()
            xcopies.append(copy)

    node_grad = mm_t(ya[:own_rows], wa) + mm_t(yb[:own_rows], wb)
    grad_part[...] = cot[...].astype(F32) + node_grad.reshape(NBD, BLOCK, D)
    value = q[:, x].astype(F32)
    for copy in xcopies:
        copy.wait_recv()
    for d in range(NX - 1):
        value = value + xbuf[d].astype(F32)
    r[...] = value.astype(BF16)
    ycopies = []
    for d, peer in enumerate(ypeers):
        copy = remote(r.at[lax.rem(y + d + 1, NY)], ybuf.at[d], y2s.at[d], y2r.at[d], peer)
        copy.start()
        ycopies.append(copy)

    for copy in backs:
        copy.wait_recv()
    owner = (sf[0], sf[1], sd[0], sd[1])

    def settle(k, part, out):
        for b in range(NBD):
            value = part[b]
            for s in range(NH):
                value = value + jnp.where(owner[s] == b, got[s, k].astype(F32), 0.0)
            out[b] = value.astype(BF16)

    settle(0, state_part, new_state)
    stores[1].start()

    value = r[y].astype(F32)
    for d, copy in enumerate(ycopies):
        copy.wait_recv()
        value = value + ybuf[d].astype(F32)
    t[...] = value.astype(BF16)

    copy_z = remote(t, zbuf.at[z], z2s, z2r.at[z], (a, y * NZ + a))

    @pl.when(z != a)
    def _():
        copy_z.start()

    settle(1, grad_part, grad_state)
    stores[2].start()

    fcopies = [
        remote(fin, finbuf, fs.at[d], fr, peer) for d, peer in enumerate(dpeers)
    ]

    @pl.when(z == a)
    def _():
        acc = t[...].astype(F32)
        for d in range(1, NZ):
            zz = lax.rem(z + d, NZ)
            remote(t, zbuf.at[zz], z2s, z2r.at[zz], sib).wait_recv()
            acc = acc + zbuf[zz].astype(F32)
        fin[...] = acc.astype(BF16)
        for copy in fcopies:
            copy.start()
        total[...] = fin[...].astype(F32)
        for copy in fcopies:
            copy.wait_send()

    @pl.when(z != a)
    def _():
        remote(fin, finbuf, fs.at[0], fr, sib).wait_recv()
        total[...] = finbuf[...].astype(F32)
        copy_z.wait_send()

    @pl.when(zc == c)
    def _():
        for copy in zcopies:
            copy.wait_send()

    stores[3].start()
    for copy in sent + halos + backs + cores + xcopies + ycopies:
        copy.wait_send()
    for copy in stores:
        copy.wait()


def layer(near, far, sf, sd, w1, w2, w3, node, cot, edge):
    hbm = pl.BlockSpec(memory_space=pltpu.HBM)
    dma = pltpu.SemaphoreType.DMA
    steps, rows = PAIRS // CHUNK, CHUNK * BLOCK
    shard = (UNITS, 8, D)

    def smem(count):
        return pltpu.SMEM((count,), jnp.int32)

    def bf(*shape):
        return pltpu.VMEM(shape, BF16)

    def f32(*shape):
        return pltpu.VMEM(shape, F32)

    lent = bf(NH, 2, BLOCK, D)
    blocks = f32(NBD, BLOCK, D)
    return pl.pallas_call(
        layer_kernel,
        out_shape=(
            jax.ShapeDtypeStruct(node.shape, BF16),
            jax.ShapeDtypeStruct(cot.shape, BF16),
            jax.ShapeDtypeStruct(edge.shape, BF16),
            jax.ShapeDtypeStruct(shard, F32),
        ),
        in_specs=[hbm] * 10,
        out_specs=(hbm,) * 4,
        scratch_shapes=[
            smem(PAIRS), smem(PAIRS), smem(2), smem(2), smem(2 * PAIRS), smem(NEXT),
            bf(*w1.shape), bf(*w2.shape), bf(*w3.shape), bf(*node.shape), bf(*cot.shape), bf(*edge.shape),
            lent, bf(NY, NZH, 2, *shard), lent,
            bf(3 * D, D), bf(3 * D, D), bf(D, D), bf(D, D), bf(D, D),
            f32(NEXT, BLOCK, D), f32(NEXT, BLOCK, D), bf(NEXT, BLOCK, D),
            f32(2 * PAIRS + 1, BLOCK, D), f32(2, 2 * PAIRS + 1, BLOCK, D),
            bf(steps, 2 * rows, D), f32(2 * rows, D), bf(steps, rows, D), bf(steps, 2 * rows, D),
            bf(steps, rows, D), bf(steps, rows, D),
            f32(3 * D, D), bf(NY, NZH, 2, *shard), lent, blocks, blocks,
            lent, bf(NY, NZH, *shard), bf(NY, NZH, *shard), bf(NX - 1, NY, *shard), bf(NY, *shard),
            bf(NY - 1, *shard), bf(*shard), bf(NZ, *shard), bf(*shard), bf(*shard),
            bf(*node.shape), bf(*cot.shape), bf(*edge.shape), f32(*shard),
            dma((4,)), dma((10,)), dma((NZ - 1,)), dma((NZH,)), dma((NZH, NY - 1)), dma((NY, NZH)),
            dma((NY * NZH,)), dma((NY, NZH)), dma((NH,)), dma((NH,)), dma((NH,)), dma((NH,)),
            dma((2,)), dma((2,)), dma((2, NX - 1)), dma((2, NX - 1)),
            dma((NY - 1,)), dma((NY - 1,)), dma, dma((NZ,)), dma((2 * NX - 1,)), dma,
        ],
        compiler_params=pltpu.CompilerParams(
            collective_id=0, has_side_effects=True, vmem_limit_bytes=VMEM_MIB << 20
        ),
        name="layer",
    )(near, far, sf, sd, w1, w2, w3, node, cot, edge)


def results_kernel(
    state, grad, edges, total, out_state, out_grad, out_edges, out_1, out_2, out_3,
    state_v, grad_v, edges_v, total_v, in_sem, out_sem,
):
    quarter = edges.shape[0] // 4
    spans = [pl.ds(i * quarter, quarter) for i in range(4)]
    loads, stores = [], []
    for i, (src, held, parts) in enumerate([
        (edges.at[s], edges_v.at[s], [(edges_v.at[s], out_edges.at[s])]) for s in spans
    ] + [
        (state, state_v, [(state_v, out_state)]),
        (grad, grad_v, [(grad_v, out_grad)]),
        (total, total_v, [(total_v.at[0:3], out_1), (total_v.at[3], out_2), (total_v.at[4], out_3)]),
    ]):
        loads.append(pltpu.make_async_copy(src, held, in_sem.at[i]))
        stores.append([pltpu.make_async_copy(p, q, out_sem.at[i + k]) for k, (p, q) in enumerate(parts)])
    for load in loads:
        load.start()
    for load, parts in zip(loads, stores):
        load.wait()
        for store in parts:
            store.start()
    for parts in stores:
        for store in parts:
            store.wait()


def results(state, grad, edges, total):
    hbm = pl.BlockSpec(memory_space=pltpu.HBM)
    dma = pltpu.SemaphoreType.DMA
    return pl.pallas_call(
        results_kernel,
        out_shape=(
            jax.ShapeDtypeStruct(state.shape, BF16),
            jax.ShapeDtypeStruct(grad.shape, BF16),
            jax.ShapeDtypeStruct(edges.shape, BF16),
            jax.ShapeDtypeStruct((3, 8, D), F32),
            jax.ShapeDtypeStruct((8, D), F32),
            jax.ShapeDtypeStruct((8, D), F32),
        ),
        in_specs=[hbm] * 4,
        out_specs=(hbm,) * 6,
        scratch_shapes=[
            pltpu.VMEM(state.shape, BF16), pltpu.VMEM(grad.shape, BF16),
            pltpu.VMEM(edges.shape, BF16), pltpu.VMEM(total.shape, F32),
            dma((7,)), dma((9,)),
        ],
        compiler_params=pltpu.CompilerParams(vmem_limit_bytes=VMEM_MIB << 20),
        name="results",
    )(state, grad, edges, total)


def body(node_state, edge_state, cotangent, w_first, w_second, w_third,
         pair_near, pair_far, send_fsdp, send_dom):
    new_state, grad_state, grad_edges, total = layer(
        pair_near, pair_far, send_fsdp.reshape(2), send_dom.reshape(2), w_first, w_second, w_third,
        node_state.reshape(NBD, BLOCK, D), cotangent.reshape(NBD, BLOCK, D), edge_state,
    )
    new_state, grad_state, grad_edges, g1, g2, g3 = results(new_state, grad_state, grad_edges, total)
    return (
        new_state.reshape(NBD * BLOCK, D),
        grad_state.reshape(NBD * BLOCK, D),
        grad_edges,
        g1.reshape(24, D),
        g2,
        g3,
    )


def solution(mesh):
    cells = P(("dom", "fsdp"), None)
    rows = P("fsdp", None)
    flat = P(("dom", "fsdp"))
    lists = P(("dom", "fsdp"), None, None)
    return jax.shard_map(
        body,
        mesh=mesh,
        in_specs=(cells, cells, cells, rows, rows, rows, flat, flat, lists, lists),
        out_specs=(cells, cells, cells, rows, rows, rows),
        check_vma=False,
    )
```

time: 66.4 us -> 52.8 us (0.80)
  local copies, waits for them, and re-layouts: 8.63 us -> 0 us
  Pallas kernels: 56 us -> 51.2 us
    unnamed x26 -> x0, local copies, waits for them, and re-layouts: 7.41 us -> none
    pallas_call x3 -> x2, Pallas kernels: 56 us -> 51.2 us  [the longest x1 48.9 us: layer(): pl.pallas_call(layer_kernel, out_shape=(jax.ShapeDtypeStruct(node.shape,...]
where the time goes in v2:
time: 52.8 us; the launch traced here: 51.9 us
  Pallas kernels  51.2 us (97%)
  between operations  0.64 us (1%)
    pallas_call x1, Pallas kernels, layer(): pl.pallas_call(layer_kernel, out_shape=(jax.ShapeDtypeStruct(node.shape,...  48.9 us
    pallas_call x1, Pallas kernels, results(): pl.pallas_call(results_kernel, out_shape=(jax.ShapeDtypeStruct(state.shap...  2.34 us

profile of v2, /device:TPU:1, one launch (start us, length us, event | category | flops | bytes accessed | tf_op | source)
XLA Modules:
  0.0 51.9 jit_solution(9678490703046552738)
XLA Ops:
  0.6 48.9 %layer.1 = (bf16[6,128,256]{2,1,0:T(8,128)(2,1)}, bf16[6,128,256]{2,1,0:T(8,128)(2,1)}, bf16[2048,256]{1,0:T(8,128)(2,1)}, f32[5,8,256]{2,1,0:T(8,128)}) custom-call(s32[16]{0:T(128)} %near_hbm.1, s32[16]{0:T(128)} %far_hbm.1, s32[2]{0:T(128)} %bitcast.9, s32[2]{0:T(128)} %bitcast.10, bf16[24,256]{1,0:T(8,128)(2,1)} %w1_hbm.1, bf16[8,256]{1,0:T(8,128)(2,1)} %w2_hbm.1, ...), custom_call_target="tpu_custom_call" | custom-call | tf_op jit(solution)/shard_map/layer/pallas_call | solution.py:423
  49.5 2.3 %results.1 = (bf16[6,128,256]{2,1,0:T(8,128)(2,1)}, bf16[6,128,256]{2,1,0:T(8,128)(2,1)}, bf16[2048,256]{1,0:T(8,128)(2,1)}, f32[3,8,256]{2,1,0:T(8,128)}, f32[8,256]{1,0:T(8,128)}, /*index=5*/f32[8,256]{1,0:T(8,128)}) custom-call(bf16[6,128,256]{2,1,0:T(8,128)(2,1)} %get-tuple-element.16.state, bf16[6,128,256]{2,1,0:T(8,128)(2,1)} %get-tuple-element.17.grad, ...), custom_call_target="tpu_custom_call" | custom-call | tf_op jit(solution)/shard_map/results/pallas_call | solution.py:488

commit v3 on v2

v3 whole, which is shorter than its diff:
```python
import jax
import jax.numpy as jnp
from jax import lax
from jax.experimental import pallas as pl
from jax.experimental.pallas import tpu as pltpu
from jax.sharding import PartitionSpec as P

BLOCK = 128
D = 256
NBD = 6
NH = 4
NEXT = NBD + NH
PAIRS = 16
NX, NY, NZ = 4, 4, 8
NZH = NZ // 2
UNITS = 5
CHUNK = 4
UNROLL = True
VMEM_MIB = 58
LENT_CHUNK = 2
MESH = pl.DeviceIdType.MESH
F32, BF16 = jnp.float32, jnp.bfloat16


def place():
    a = lax.axis_index("dom")
    f = lax.axis_index("fsdp")
    return a, f, a // 2, lax.rem(a, 2), f // NZ, lax.rem(f, NZ)


def halo_peers(a, f):
    nd, nf = 2 * NX, NY * NZ
    return (
        (a, lax.rem(f + nf - 1, nf)),
        (a, lax.rem(f + 1, nf)),
        (lax.rem(a + nd - 1, nd), f),
        (lax.rem(a + 1, nd), f),
    )


def signal_all(peers):
    barrier = pltpu.get_barrier_semaphore()
    for peer in peers:
        pl.semaphore_signal(barrier, inc=1, device_id=peer, device_id_type=MESH)


def wait_all(count):
    pl.semaphore_wait(pltpu.get_barrier_semaphore(), count)


def remote(src, dst, send, recv, peer):
    return pltpu.make_async_remote_copy(
        src_ref=src, dst_ref=dst, send_sem=send, recv_sem=recv,
        device_id=peer, device_id_type=MESH,
    )


def mm(p, q):
    return jnp.dot(p, q, preferred_element_type=F32)


def mm_t(p, q):
    return lax.dot_general(p, q, (((1,), (1,)), ((), ())), preferred_element_type=F32)


def t_mm(p, q):
    return lax.dot_general(p, q, (((0,), (0,)), ((), ())), preferred_element_type=F32)


def act_slope(half):
    up = 1.0 + jnp.tanh(half)
    act = half * up
    return act, up + act * (2.0 - up)


def layer_kernel(
    near_hbm, far_hbm, sf_hbm, sd_hbm, w1_hbm, w2_hbm, w3_hbm, node_hbm, cot_hbm, edge_hbm,
    state_out, grad_out, edge_out, pieces_out, order_out,
    near_in, far_in, sf, sd, order, near, far, chain, last, w1s, w2s, w3s, node, cot, edge_in, edge, lend, wall, halo,
    w1, w1h, w2h, w3, w3h, left, right, ctab, tsum, ysum, a1, d1, gg, sg, dd, ef,
    first, acc_2, acc_3, grads, back, state_part, grad_part,
    got, sibbuf, q, ybuf, r, zbuf, fin, new_state, grad_state, ge,
    os, ls, zs, zr, ys, yr, ss, sr, hs, hr, bs, br, s0, r0, y2s, y2r, z2s, z2r, fs, fr,
):
    a, f, x, c, y, z = place()
    zh, zc = z // 2, lax.rem(z, 2)
    sib = (a + 1 - 2 * c, f)
    ypeers = [(a, lax.rem(y + d, NY) * NZ + z) for d in range(1, NY)]
    zpeers = [(a, y * NZ + lax.rem(z + d, NZ)) for d in range(1, NZ)]
    dpeers = [(lax.rem(a + d, 2 * NX), f) for d in range(1, 2 * NX)]
    hpeers = halo_peers(a, f)
    everyone = zpeers + ypeers + dpeers + list(hpeers)
    signal_all(everyone)

    loads = [
        pltpu.make_async_copy(src, dst, ls.at[i])
        for i, (src, dst) in enumerate((
            (w1_hbm, w1s), (w2_hbm, w2s), (w3_hbm, w3s), (sf_hbm, sf), (sd_hbm, sd),
            (node_hbm, node), (cot_hbm, cot), (near_hbm, near_in), (far_hbm, far_in), (edge_hbm, edge_in),
        ))
    ]
    for copy in loads:
        copy.start()
    for copy in loads[:3]:
        copy.wait()

    @pl.when(zc == c)
    def _():
        wall[y, zh, c, 0:3] = w1s[...].astype(F32).reshape(3, 8, D).astype(BF16)
        wall[y, zh, c, 3] = w2s[...]
        wall[y, zh, c, 4] = w3s[...]

    for copy in loads[3:7]:
        copy.wait()
    for s in range(2):
        b = sf[s]
        lend[s, 0] = node[b]
        lend[s, 1] = cot[b]
        b = sd[s]
        lend[2 + s, 0] = node[b]
        lend[2 + s, 1] = cot[b]
    wait_all(len(everyone))

    halos = [
        remote(lend.at[s], halo.at[s ^ 1], hs.at[s], hr.at[s ^ 1], hpeers[s])
        for s in range(NH)
    ]
    zcopies = [
        remote(wall.at[y, zh, c], wall.at[y, zh, c], zs.at[d], zr.at[zh], zpeers[d])
        for d in (3, 2, 4, 1, 5, 0, 6)
    ]

    @pl.when(zc == c)
    def _():
        for copy in zcopies:
            copy.start()

    halos[2].start()
    halos[3].start()

    loads[7].wait()
    loads[8].wait()
    count, place_of = jnp.int32(0), []
    for p in range(PAIRS):
        entry = far_in[p]
        own_place = count + jnp.where(count < LENT_CHUNK * CHUNK, 0, CHUNK)
        place_of.append(jnp.where(entry < NBD, own_place, entry + (LENT_CHUNK * CHUNK - NBD)))
        count = count + jnp.where(entry < NBD, 1, 0)

    def arrange(i, carry):
        pair, near_i, far_i = jnp.int32(0), near_in[0], far_in[0]
        for p in range(1, PAIRS):
            here = place_of[p] == i
            pair = jnp.where(here, p, pair)
            near_i = jnp.where(here, near_in[p], near_i)
            far_i = jnp.where(here, far_in[p], far_i)
        order[i] = pair
        near[i] = near_i
        far[i] = far_i
        return carry

    lax.fori_loop(0, PAIRS, arrange, 0)

    keys = [(near, far)[h % 2][h // 2] for h in range(2 * PAIRS)]

    def link(h, carry):
        p = h // 2
        key = jnp.where(lax.rem(h, 2) == 0, near[p], far[p])
        before = jnp.int32(2 * PAIRS)
        for g in range(2 * PAIRS):
            before = jnp.where((keys[g] == key) & (g < h), g, before)
        chain[h] = before
        return carry

    lax.fori_loop(0, 2 * PAIRS, link, 0)

    def end(b, carry):
        where = jnp.int32(2 * PAIRS)
        for g in range(2 * PAIRS):
            where = jnp.where(keys[g] == b, g, where)
        last[b] = where
        return carry

    lax.fori_loop(0, NEXT, end, 0)

    sent = []

    def pass_on(yy, h, slot, along_y):
        part = wall.at[yy, h, c]
        if along_y:
            for d, peer in enumerate(ypeers):
                copy = remote(part, part, ys.at[slot, d], yr.at[y, h], peer)
                copy.start()
                sent.append(copy)
        copy = remote(part, part, ss.at[slot], sr.at[yy, h], sib)
        copy.start()
        sent.append(copy)

    for i, d in enumerate((0, 1, 3, 2)):
        h = lax.rem(zh + d, NZH)

        @pl.when(2 * h + c != z)
        def _():
            part = wall.at[y, h, c]
            remote(part, part, zs.at[0], zr.at[h], sib).wait_recv()

        pass_on(y, h, i, True)

    tsum[2 * PAIRS] = jnp.zeros((BLOCK, D), F32)
    ysum[0, 2 * PAIRS] = jnp.zeros((BLOCK, D), F32)
    ysum[1, 2 * PAIRS] = jnp.zeros((BLOCK, D), F32)
    ctab[0:NBD] = cot[...]

    for i, d in enumerate((0, 1, 3, 2)):
        h = lax.rem(zh + d, NZH)
        for e in (1, 3, 2):
            yy = lax.rem(y + e, NY)
            part = wall.at[yy, h, c]
            remote(part, part, ys.at[0, 0], yr.at[yy, h], sib).wait_recv()
            pass_on(yy, h, 4 * e + i, False)
    halos[0].start()
    halos[1].start()
    loads[9].wait()
    rows = CHUNK * BLOCK
    direct = [slice(j * BLOCK, (j + 1) * BLOCK) for j in range(CHUNK)]
    mirror = [slice(rows + j * BLOCK, rows + (j + 1) * BLOCK) for j in range(CHUNK)]
    own_rows = NBD * BLOCK
    for yy in range(NY):
        for h in range(NZH):
            part = wall.at[yy, h, 1 - c]
            remote(part, part, ss.at[0], sr.at[yy, h], sib).wait_recv()

    packed = wall[...].reshape(NY * NZ, UNITS, 8, D).astype(F32)
    flat = packed[:, 0:3].reshape(3 * D, D)
    w1[...] = flat.astype(BF16)
    w1h[...] = (0.5 * flat).astype(BF16)
    w2h[...] = (0.5 * packed[:, 3].reshape(D, D)).astype(BF16)
    third = packed[:, 4].reshape(D, D)
    w3[...] = third.astype(BF16)
    w3h[...] = (0.5 * third).astype(BF16)
    own = node[...].reshape(own_rows, D)
    for table, cols in ((left, 0), (right, D)):
        table[0:NBD] = mm(own, w1h[cols:cols + D]).reshape(NBD, BLOCK, D)

    def part_of(ref, steps):
        return ref[0:steps].reshape(-1, D)

    def chunk(i, carry):
        pairs = [i * CHUNK + j for j in range(CHUNK)]
        ends = [(near[p], far[p]) for p in pairs]
        links = [(2 * p, chain[2 * p], chain[2 * p + 1]) for p in pairs]
        span = pl.ds(pl.multiple_of(i * rows, rows), rows)
        for j, p in enumerate(pairs):
            edge[pl.ds(pl.multiple_of(p * BLOCK, BLOCK), BLOCK)] = edge_in[order[p]]
        edge_part = mm(edge[span], w1h[2 * D:])
        for j, (n, m) in enumerate(ends):
            gg[i, direct[j]] = (ctab[n].astype(F32) - ctab[m].astype(F32)).astype(BF16)
            for where, p, k in ((direct[j], n, m), (mirror[j], m, n)):
                act, slope = act_slope(left[p] + right[k] + edge_part[direct[j]])
                a1[i, where] = act.astype(BF16)
                d1[where] = slope
        second = mm(a1[i], w2h[...])
        back_3 = mm_t(gg[i], w3h[...])
        for j, (h, before_n, before_m) in enumerate(links):
            act_f, slope_f = act_slope(second[direct[j]])
            act_m, slope_m = act_slope(second[mirror[j]])
            diff = act_f - act_m
            dd[i, direct[j]] = diff.astype(BF16)
            tsum[h] = tsum[before_n] + diff
            tsum[h + 1] = tsum[before_m] - diff
            sg[i, direct[j]] = (back_3[direct[j]] * slope_f).astype(BF16)
            sg[i, mirror[j]] = (-back_3[direct[j]] * slope_m).astype(BF16)
        first_back = mm_t(sg[i], w2h[...])
        for j, (h, before_n, before_m) in enumerate(links):
            part_f = first_back[direct[j]] * d1[direct[j]]
            part_m = first_back[mirror[j]] * d1[mirror[j]]
            ef[i, direct[j]] = (part_f + part_m).astype(BF16)
            ysum[0, h] = ysum[0, before_n] + part_f
            ysum[0, h + 1] = ysum[0, before_m] + part_m
            ysum[1, h] = ysum[1, before_n] + part_m
            ysum[1, h + 1] = ysum[1, before_m] + part_f
        ge[span] = mm_t(ef[i], w1[2 * D:]).astype(BF16)
        return carry

    final = PAIRS // CHUNK - 1
    lax.fori_loop(0, LENT_CHUNK, chunk, 0, unroll=UNROLL)

    for s in range(NH):
        halos[s].wait_recv()
    ctab[NBD:] = halo[:, 1]
    lent = halo[:, 0].reshape(NH * BLOCK, D)
    for table, cols in ((left, 0), (right, D)):
        table[NBD:] = mm(lent, w1h[cols:cols + D]).reshape(NH, BLOCK, D)
    chunk(LENT_CHUNK, 0)

    wa, wb = w1[0:D], w1[D:2 * D]
    lent_ends = [2 * (LENT_CHUNK * CHUNK + k) + 1 for k in range(NH)]

    def lent_sum(ref):
        return jnp.concatenate([ref[h].astype(BF16) for h in lent_ends], 0)

    lent_flux = mm(lent_sum(tsum), w3[...])
    lent_grad = mm_t(lent_sum(ysum.at[0]), wa) + mm_t(lent_sum(ysum.at[1]), wb)
    back[:, 0] = lent_flux.astype(BF16).reshape(NH, BLOCK, D)
    back[:, 1] = lent_grad.astype(BF16).reshape(NH, BLOCK, D)
    backs = [
        remote(back.at[s], got.at[s ^ 1], bs.at[s], br.at[s ^ 1], hpeers[s])
        for s in range(NH)
    ]
    for copy in backs:
        copy.start()

    lax.fori_loop(LENT_CHUNK + 1, PAIRS // CHUNK, chunk, 0, unroll=UNROLL)
    first[2 * D:] = t_mm(edge[0:final * rows], part_of(ef, final))
    acc_2[...] = t_mm(part_of(a1, final), part_of(sg, final))
    acc_3[...] = t_mm(part_of(dd, final), part_of(gg, final))
    stores = [
        pltpu.make_async_copy(src, dst, os.at[i])
        for i, (src, dst) in enumerate((
            (ge, edge_out), (new_state, state_out), (grad_state, grad_out),
        ))
    ]
    stores[0].start()
    order_store = pltpu.make_async_copy(order, order_out, os.at[4])
    order_store.start()

    ends = [last[b] for b in range(NEXT)]

    def gathered(pick):
        return jnp.concatenate([pick(h).astype(BF16) for h in ends], 0)

    ts = gathered(lambda h: tsum[h])
    ya = gathered(lambda h: ysum[0, h])
    yb = gathered(lambda h: ysum[1, h])

    pieces = (slice(3, 5), slice(0, 3))

    def to_sibling(k):
        copy = remote(grads.at[:, :, 1 - c, pieces[k]], sibbuf.at[:, :, pieces[k]], s0.at[k], r0.at[k], sib)
        copy.start()
        return copy

    grads[:, :, :, 3] = (acc_2[...] + t_mm(a1[final], sg[final])).reshape(NY, NZH, 2, 8, D).astype(BF16)
    grads[:, :, :, 4] = (acc_3[...] + t_mm(dd[final], gg[final])).reshape(NY, NZH, 2, 8, D).astype(BF16)
    cores = [to_sibling(0)]
    first[0:D] = t_mm(own, ya[:own_rows]) + t_mm(lent, ya[own_rows:])
    first[D:2 * D] = t_mm(own, yb[:own_rows]) + t_mm(lent, yb[own_rows:])
    first[2 * D:] += t_mm(edge[final * rows:], ef[final])
    grads[:, :, :, 0:3] = first[...].reshape(NY, NZH, 2, 3, 8, D).astype(BF16)
    cores.append(to_sibling(1))

    ycopies = []
    for k, piece in enumerate(pieces):
        cores[k].wait_recv()
        q[:, :, piece] = (grads[:, :, c, piece].astype(F32) + sibbuf[:, :, piece].astype(F32)).astype(BF16)
        for d, peer in enumerate(ypeers):
            yy = lax.rem(y + d + 1, NY)
            copy = remote(q.at[yy, :, piece], ybuf.at[d, :, piece], y2s.at[k, d], y2r.at[k, d], peer)
            copy.start()
            ycopies.append(copy)

    flux = mm(ts[:own_rows], w3[...]).reshape(NBD, BLOCK, D)
    state_part[...] = node[...].astype(F32) + flux
    node_grad = mm_t(ya[:own_rows], wa) + mm_t(yb[:own_rows], wb)
    grad_part[...] = cot[...].astype(F32) + node_grad.reshape(NBD, BLOCK, D)

    value = q[y].astype(F32)
    for copy in ycopies:
        copy.wait_recv()
    for d in range(NY - 1):
        value = value + ybuf[d].astype(F32)
    r[...] = value.astype(BF16)

    rcopies = []
    for k, d in enumerate((2, 1, 3, 0)):
        h = lax.rem(zh + d, NZH)
        copy = remote(r.at[h], zbuf.at[z], z2s.at[k], z2r.at[z], (a, y * NZ + 2 * h + c))
        rcopies.append((h, copy))

        @pl.when(2 * h + c != z)
        def _():
            copy.start()

    for copy in backs:
        copy.wait_recv()
    owner = (sf[0], sf[1], sd[0], sd[1])

    def settle(k, part, out):
        for b in range(NBD):
            value = part[b]
            for s in range(NH):
                value = value + jnp.where(owner[s] == b, got[s, k].astype(F32), 0.0)
            out[b] = value.astype(BF16)

    settle(0, state_part, new_state)
    stores[1].start()
    settle(1, grad_part, grad_state)
    stores[2].start()

    fcopies = [
        remote(fin, pieces_out.at[x], fs.at[d], fr.at[x], dpeers[d]) for d in (3, 4, 2, 5, 1, 6, 0)
    ]

    @pl.when(zc == c)
    def _():
        acc = r[zh].astype(F32)
        for d in (1, 7, 2, 6, 3, 5, 4):
            zz = lax.rem(z + d, NZ)
            remote(r.at[0], zbuf.at[zz], z2s.at[0], z2r.at[zz], sib).wait_recv()
            acc = acc + zbuf[zz].astype(F32)
        fin[...] = acc.astype(BF16)
        for copy in fcopies:
            copy.start()
        own_piece = pltpu.make_async_copy(fin, pieces_out.at[x], os.at[3])
        own_piece.start()
        for copy in fcopies:
            copy.wait_send()
        own_piece.wait()

    @pl.when(zc != c)
    def _():
        remote(fin, pieces_out.at[x], fs.at[0], fr.at[x], sib).wait_recv()

    for d in range(1, NX):
        xx = lax.rem(x + d, NX)
        remote(fin, pieces_out.at[xx], fs.at[0], fr.at[xx], sib).wait_recv()

    for h, copy in rcopies:
        @pl.when(2 * h + c != z)
        def _():
            copy.wait_send()

    @pl.when(zc == c)
    def _():
        for copy in zcopies:
            copy.wait_send()

    for copy in sent + halos + backs + cores + ycopies:
        copy.wait_send()
    for copy in stores + [order_store]:
        copy.wait()


def layer(near, far, sf, sd, w1, w2, w3, node, cot, edge):
    hbm = pl.BlockSpec(memory_space=pltpu.HBM)
    dma = pltpu.SemaphoreType.DMA
    steps, rows = PAIRS // CHUNK, CHUNK * BLOCK
    shard = (UNITS, 8, D)

    def smem(count):
        return pltpu.SMEM((count,), jnp.int32)

    def bf(*shape):
        return pltpu.VMEM(shape, BF16)

    def f32(*shape):
        return pltpu.VMEM(shape, F32)

    lent = bf(NH, 2, BLOCK, D)
    blocks = f32(NBD, BLOCK, D)
    return pl.pallas_call(
        layer_kernel,
        out_shape=(
            jax.ShapeDtypeStruct(node.shape, BF16),
            jax.ShapeDtypeStruct(cot.shape, BF16),
            jax.ShapeDtypeStruct((PAIRS * BLOCK, D), BF16),
            jax.ShapeDtypeStruct((NX, *shard), BF16),
            jax.ShapeDtypeStruct((PAIRS,), jnp.int32),
        ),
        in_specs=[hbm] * 10,
        out_specs=(hbm,) * 5,
        scratch_shapes=[
            smem(PAIRS), smem(PAIRS), smem(2), smem(2), smem(PAIRS), smem(PAIRS), smem(PAIRS), smem(2 * PAIRS), smem(NEXT),
            bf(*w1.shape), bf(*w2.shape), bf(*w3.shape), bf(*node.shape), bf(*cot.shape), bf(*edge.shape), bf(PAIRS * BLOCK, D),
            lent, bf(NY, NZH, 2, *shard), lent,
            bf(3 * D, D), bf(3 * D, D), bf(D, D), bf(D, D), bf(D, D),
            f32(NEXT, BLOCK, D), f32(NEXT, BLOCK, D), bf(NEXT, BLOCK, D),
            f32(2 * PAIRS + 1, BLOCK, D), f32(2, 2 * PAIRS + 1, BLOCK, D),
            bf(steps, 2 * rows, D), f32(2 * rows, D), bf(steps, rows, D), bf(steps, 2 * rows, D),
            bf(steps, rows, D), bf(steps, rows, D),
            f32(3 * D, D), f32(D, D), f32(D, D), bf(NY, NZH, 2, *shard), lent, blocks, blocks,
            lent, bf(NY, NZH, *shard), bf(NY, NZH, *shard), bf(NY - 1, NZH, *shard), bf(NZH, *shard),
            bf(NZ, *shard), bf(*shard),
            bf(*node.shape), bf(*cot.shape), bf(PAIRS * BLOCK, D),
            dma((5,)), dma((10,)), dma((NZ - 1,)), dma((NZH,)), dma((NZH, NY - 1)), dma((NY, NZH)),
            dma((NY * NZH,)), dma((NY, NZH)), dma((NH,)), dma((NH,)), dma((NH,)), dma((NH,)),
            dma((2,)), dma((2,)), dma((2, NY - 1)), dma((2, NY - 1)),
            dma((NZH,)), dma((NZ,)), dma((2 * NX - 1,)), dma((NX,)),
        ],
        compiler_params=pltpu.CompilerParams(
            collective_id=0, has_side_effects=True, vmem_limit_bytes=VMEM_MIB << 20
        ),
        name="layer",
    )(near, far, sf, sd, w1, w2, w3, node, cot, edge)


def results_kernel(
    order_hbm, state, grad, edges, total, out_state, out_grad, out_edges, out_1, out_2, out_3,
    order, state_v, grad_v, edges_v, sum_v, total_v, order_sem, in_sem, out_sem,
):
    order_copy = pltpu.make_async_copy(order_hbm, order, order_sem)
    order_copy.start()
    quarter = CHUNK * BLOCK
    spans = [pl.ds(i * quarter, quarter) for i in range(PAIRS // CHUNK)]
    loads = [
        pltpu.make_async_copy(src, held, in_sem.at[i])
        for i, (src, held) in enumerate(
            [(edges.at[s], edges_v.at[s]) for s in spans]
            + [(state, state_v), (grad, grad_v), (total, sum_v)]
        )
    ]
    for load in loads:
        load.start()
    order_copy.wait()
    stores = []

    def store(src, dst):
        copy = pltpu.make_async_copy(src, dst, out_sem.at[len(stores)])
        copy.start()
        stores.append(copy)

    for i in range(PAIRS):
        if i % CHUNK == 0:
            loads[i // CHUNK].wait()
        rows = pl.ds(pl.multiple_of(order[i] * BLOCK, BLOCK), BLOCK)
        store(edges_v.at[pl.ds(i * BLOCK, BLOCK)], out_edges.at[rows])
    loads[4].wait()
    store(state_v, out_state)
    loads[5].wait()
    store(grad_v, out_grad)
    loads[6].wait()
    total_v[...] = sum((sum_v[i].astype(F32) for i in range(1, NX)), sum_v[0].astype(F32))
    store(total_v.at[0:3], out_1)
    store(total_v.at[3], out_2)
    store(total_v.at[4], out_3)
    for copy in stores:
        copy.wait()


def results(order, state, grad, edges, total):
    hbm = pl.BlockSpec(memory_space=pltpu.HBM)
    dma = pltpu.SemaphoreType.DMA
    return pl.pallas_call(
        results_kernel,
        out_shape=(
            jax.ShapeDtypeStruct(state.shape, BF16),
            jax.ShapeDtypeStruct(grad.shape, BF16),
            jax.ShapeDtypeStruct(edges.shape, BF16),
            jax.ShapeDtypeStruct((3, 8, D), F32),
            jax.ShapeDtypeStruct((8, D), F32),
            jax.ShapeDtypeStruct((8, D), F32),
        ),
        in_specs=[hbm] * 5,
        out_specs=(hbm,) * 6,
        scratch_shapes=[
            pltpu.SMEM((PAIRS,), jnp.int32),
            pltpu.VMEM(state.shape, BF16), pltpu.VMEM(grad.shape, BF16),
            pltpu.VMEM(edges.shape, BF16), pltpu.VMEM(total.shape, BF16), pltpu.VMEM(total.shape[1:], F32),
            dma, dma((7,)), dma((PAIRS + 5,)),
        ],
        compiler_params=pltpu.CompilerParams(vmem_limit_bytes=VMEM_MIB << 20),
        name="results",
    )(order, state, grad, edges, total)


def body(node_state, edge_state, cotangent, w_first, w_second, w_third,
         pair_near, pair_far, send_fsdp, send_dom):
    new_state, grad_state, grad_edges, total, order = layer(
        pair_near, pair_far, send_fsdp.reshape(2), send_dom.reshape(2), w_first, w_second, w_third,
        node_state.reshape(NBD, BLOCK, D), cotangent.reshape(NBD, BLOCK, D),
        edge_state.reshape(PAIRS, BLOCK, D),
    )
    new_state, grad_state, grad_edges, g1, g2, g3 = results(
        order, new_state, grad_state, grad_edges, total
    )
    return (
        new_state.reshape(NBD * BLOCK, D),
        grad_state.reshape(NBD * BLOCK, D),
        grad_edges,
        g1.reshape(24, D),
        g2,
        g3,
    )


def solution(mesh):
    cells = P(("dom", "fsdp"), None)
    rows = P("fsdp", None)
    flat = P(("dom", "fsdp"))
    lists = P(("dom", "fsdp"), None, None)
    return jax.shard_map(
        body,
        mesh=mesh,
        in_specs=(cells, cells, cells, rows, rows, rows, flat, flat, lists, lists),
        out_specs=(cells, cells, cells, rows, rows, rows),
        check_vma=False,
    )
```

time: 52.8 us -> 49.1 us (0.930); the launches traced: 51.9 us -> 49 us
  Pallas kernels: 51.2 us -> 48.3 us
    pallas_call x1, Pallas kernels: 48.9 us -> 45.9 us  [layer(): pl.pallas_call(layer_kernel, out_shape=(jax.ShapeDtypeStruct(node.shape,...]
where the time goes in v3:
time: 49.1 us; the launch traced here: 49 us
  Pallas kernels  48.3 us (98%)
  between operations  0.64 us (1%)
    pallas_call x1, Pallas kernels, layer(): pl.pallas_call(layer_kernel, out_shape=(jax.ShapeDtypeStruct(node.shape,...  45.9 us
    pallas_call x1, Pallas kernels, results(): pl.pallas_call(results_kernel, out_shape=(jax.ShapeDtypeStruct(state.shap...  2.45 us

profile of v3, /device:TPU:1, one launch (start us, length us, event | category | flops | bytes accessed | tf_op | source)
XLA Modules:
  0.0 49.0 jit_solution(9935212333254384525)
XLA Ops:
  0.6 45.9 %layer.1 = (bf16[6,128,256]{2,1,0:T(8,128)(2,1)}, bf16[6,128,256]{2,1,0:T(8,128)(2,1)}, bf16[2048,256]{1,0:T(8,128)(2,1)}, bf16[4,5,8,256]{3,2,1,0:T(8,128)(2,1)}, s32[16]{0:T(128)}) custom-call(s32[16]{0:T(128)} %near_hbm.1, s32[16]{0:T(128)} %far_hbm.1, s32[2]{0:T(128)} %bitcast.11, s32[2]{0:T(128)} %bitcast.12, bf16[24,256]{1,0:T(8,128)(2,1)} %w1_hbm.1, ...), custom_call_target="tpu_custom_call" | custom-call | tf_op jit(solution)/shard_map/layer/pallas_call | solution.py:461
  46.5 2.5 %results.1 = (bf16[6,128,256]{2,1,0:T(8,128)(2,1)}, bf16[6,128,256]{2,1,0:T(8,128)(2,1)}, bf16[2048,256]{1,0:T(8,128)(2,1)}, f32[3,8,256]{2,1,0:T(8,128)}, f32[8,256]{1,0:T(8,128)}, /*index=5*/f32[8,256]{1,0:T(8,128)}) custom-call(s32[16]{0:T(128)} %get-tuple-element.17.order_hbm, bf16[6,128,256]{2,1,0:T(8,128)(2,1)} %get-tuple-element.18.state, ...), custom_call_target="tpu_custom_call" | custom-call | tf_op jit(solution)/shard_map/results/pallas_call | solution.py:543

commit v4 on v3

--- a/solution.py
+++ b/solution.py
@@ -89,7 +89,7 @@
     zpeers = [(a, y * NZ + lax.rem(z + d, NZ)) for d in range(1, NZ)]
     dpeers = [(lax.rem(a + d, 2 * NX), f) for d in range(1, 2 * NX)]
     hpeers = halo_peers(a, f)
-    everyone = zpeers + ypeers + dpeers + list(hpeers)
+    everyone = [zpeers[d] for d in (3, 2, 4, 1, 5, 0, 6)] + ypeers + dpeers + list(hpeers[:2])
     signal_all(everyone)
 
     loads = [
@@ -364,6 +364,16 @@
     node_grad = mm_t(ya[:own_rows], wa) + mm_t(yb[:own_rows], wb)
     grad_part[...] = cot[...].astype(F32) + node_grad.reshape(NBD, BLOCK, D)
 
+    @pl.when(zc == c)
+    def _():
+        for copy in zcopies:
+            copy.wait_send()
+
+    for copy in sent + halos:
+        copy.wait_send()
+    stores[0].wait()
+    order_store.wait()
+
     value = q[y].astype(F32)
     for copy in ycopies:
         copy.wait_recv()
@@ -396,6 +406,15 @@
     stores[1].start()
     settle(1, grad_part, grad_state)
     stores[2].start()
+
+    for copy in backs + cores + ycopies:
+        copy.wait_send()
+    for h, copy in rcopies:
+        @pl.when(2 * h + c != z)
+        def _():
+            copy.wait_send()
+    for copy in stores[1:]:
+        copy.wait()
 
     fcopies = [
         remote(fin, pieces_out.at[x], fs.at[d], fr.at[x], dpeers[d]) for d in (3, 4, 2, 5, 1, 6, 0)
@@ -424,21 +443,6 @@
     for d in range(1, NX):
         xx = lax.rem(x + d, NX)
         remote(fin, pieces_out.at[xx], fs.at[0], fr.at[xx], sib).wait_recv()
-
-    for h, copy in rcopies:
-        @pl.when(2 * h + c != z)
-        def _():
-            copy.wait_send()
-
-    @pl.when(zc == c)
-    def _():
-        for copy in zcopies:
-            copy.wait_send()
-
-    for copy in sent + halos + backs + cores + ycopies:
-        copy.wait_send()
-    for copy in stores + [order_store]:
-        copy.wait()
 
 
 def layer(near, far, sf, sd, w1, w2, w3, node, cot, edge):

time: 49.1 us -> 49 us (level)
  no operation moved by 1% of the time
where the time goes in v4:
time: 49 us; the launch traced here: 48.8 us
  Pallas kernels  48.2 us (98%)
  between operations  0.64 us (1%)
    pallas_call x1, Pallas kernels, layer(): pl.pallas_call(layer_kernel, out_shape=(jax.ShapeDtypeStruct(node.shape,...  45.8 us
    pallas_call x1, Pallas kernels, results(): pl.pallas_call(results_kernel, out_shape=(jax.ShapeDtypeStruct(state.shap...  2.45 us

profile of v4, /device:TPU:1, one launch (start us, length us, event | category | flops | bytes accessed | tf_op | source)
XLA Modules:
  0.0 48.8 jit_solution(8671893718001225516)
XLA Ops:
  0.6 45.8 %layer.1 = (bf16[6,128,256]{2,1,0:T(8,128)(2,1)}, bf16[6,128,256]{2,1,0:T(8,128)(2,1)}, bf16[2048,256]{1,0:T(8,128)(2,1)}, bf16[4,5,8,256]{3,2,1,0:T(8,128)(2,1)}, s32[16]{0:T(128)}) custom-call(s32[16]{0:T(128)} %near_hbm.1, s32[16]{0:T(128)} %far_hbm.1, s32[2]{0:T(128)} %bitcast.11, s32[2]{0:T(128)} %bitcast.12, bf16[24,256]{1,0:T(8,128)(2,1)} %w1_hbm.1, ...), custom_call_target="tpu_custom_call" | custom-call | tf_op jit(solution)/shard_map/layer/pallas_call | solution.py:465
  46.4 2.5 %results.1 = (bf16[6,128,256]{2,1,0:T(8,128)(2,1)}, bf16[6,128,256]{2,1,0:T(8,128)(2,1)}, bf16[2048,256]{1,0:T(8,128)(2,1)}, f32[3,8,256]{2,1,0:T(8,128)}, f32[8,256]{1,0:T(8,128)}, /*index=5*/f32[8,256]{1,0:T(8,128)}) custom-call(s32[16]{0:T(128)} %get-tuple-element.17.order_hbm, bf16[6,128,256]{2,1,0:T(8,128)(2,1)} %get-tuple-element.18.state, ...), custom_call_target="tpu_custom_call" | custom-call | tf_op jit(solution)/shard_map/results/pallas_call | solution.py:547

commit v5 on v4

--- a/solution.py
+++ b/solution.py
@@ -258,7 +258,7 @@
             for where, p, k in ((direct[j], n, m), (mirror[j], m, n)):
                 act, slope = act_slope(left[p] + right[k] + edge_part[direct[j]])
                 a1[i, where] = act.astype(BF16)
-                d1[where] = slope
+                d1[where] = slope.astype(BF16)
         second = mm(a1[i], w2h[...])
         back_3 = mm_t(gg[i], w3h[...])
         for j, (h, before_n, before_m) in enumerate(links):
@@ -272,8 +272,8 @@
             sg[i, mirror[j]] = (-back_3[direct[j]] * slope_m).astype(BF16)
         first_back = mm_t(sg[i], w2h[...])
         for j, (h, before_n, before_m) in enumerate(links):
-            part_f = first_back[direct[j]] * d1[direct[j]]
-            part_m = first_back[mirror[j]] * d1[mirror[j]]
+            part_f = first_back[direct[j]] * d1[direct[j]].astype(F32)
+            part_m = first_back[mirror[j]] * d1[mirror[j]].astype(F32)
             ef[i, direct[j]] = (part_f + part_m).astype(BF16)
             ysum[0, h] = ysum[0, before_n] + part_f
             ysum[0, h + 1] = ysum[0, before_m] + part_m
@@ -480,7 +480,7 @@
             bf(3 * D, D), bf(3 * D, D), bf(D, D), bf(D, D), bf(D, D),
             f32(NEXT, BLOCK, D), f32(NEXT, BLOCK, D), bf(NEXT, BLOCK, D),
             f32(2 * PAIRS + 1, BLOCK, D), f32(2, 2 * PAIRS + 1, BLOCK, D),
-            bf(steps, 2 * rows, D), f32(2 * rows, D), bf(steps, rows, D), bf(steps, 2 * rows, D),
+            bf(steps, 2 * rows, D), bf(2 * rows, D), bf(steps, rows, D), bf(steps, 2 * rows, D),
             bf(steps, rows, D), bf(steps, rows, D),
             f32(3 * D, D), f32(D, D), f32(D, D), bf(NY, NZH, 2, *shard), lent, blocks, blocks,
             lent, bf(NY, NZH, *shard), bf(NY, NZH, *shard), bf(NY - 1, NZH, *shard), bf(NZH, *shard),

time: 49 us -> 49 us (level)
  no operation moved by 1% of the time
where the time goes in v5:
time: 49 us; the launch traced here: 48.9 us
  Pallas kernels  48.2 us (98%)
  between operations  0.64 us (1%)
    pallas_call x1, Pallas kernels, layer(): pl.pallas_call(layer_kernel, out_shape=(jax.ShapeDtypeStruct(node.shape,...  45.8 us
    pallas_call x1, Pallas kernels, results(): pl.pallas_call(results_kernel, out_shape=(jax.ShapeDtypeStruct(state.shap...  2.45 us

profile of v5, /device:TPU:1, one launch (start us, length us, event | category | flops | bytes accessed | tf_op | source)
XLA Modules:
  0.0 48.9 jit_solution(2370286424637070565)
XLA Ops:
  0.6 45.8 %layer.1 = (bf16[6,128,256]{2,1,0:T(8,128)(2,1)}, bf16[6,128,256]{2,1,0:T(8,128)(2,1)}, bf16[2048,256]{1,0:T(8,128)(2,1)}, bf16[4,5,8,256]{3,2,1,0:T(8,128)(2,1)}, s32[16]{0:T(128)}) custom-call(s32[16]{0:T(128)} %near_hbm.1, s32[16]{0:T(128)} %far_hbm.1, s32[2]{0:T(128)} %bitcast.11, s32[2]{0:T(128)} %bitcast.12, bf16[24,256]{1,0:T(8,128)(2,1)} %w1_hbm.1, ...), custom_call_target="tpu_custom_call" | custom-call | tf_op jit(solution)/shard_map/layer/pallas_call | solution.py:465
  46.4 2.5 %results.1 = (bf16[6,128,256]{2,1,0:T(8,128)(2,1)}, bf16[6,128,256]{2,1,0:T(8,128)(2,1)}, bf16[2048,256]{1,0:T(8,128)(2,1)}, f32[3,8,256]{2,1,0:T(8,128)}, f32[8,256]{1,0:T(8,128)}, /*index=5*/f32[8,256]{1,0:T(8,128)}) custom-call(s32[16]{0:T(128)} %get-tuple-element.17.order_hbm, bf16[6,128,256]{2,1,0:T(8,128)(2,1)} %get-tuple-element.18.state, ...), custom_call_target="tpu_custom_call" | custom-call | tf_op jit(solution)/shard_map/results/pallas_call | solution.py:547
